TPU v7x, 32 devices: a whole 2x2x4 slice. The times are simulated.
32 devices in a mesh: slab: 32 (over z, y, x, core).
Axes of the slice: x: 2, y: 2, z: 4, core: 2. Of those that a mesh axis runs over, the one named last changes fastest.
Arguments:
- coords: float32 [3, 65536], P(None, 'slab'), may hold values from -18 to 256, as said below
- charges: float32 [65536], P('slab'), may hold values from -3.6 to 3.6
- radii: float32 [65536], P('slab'), may hold values from 1.2 to 2
- screens: float32 [65536], P('slab'), may hold values from 0.6 to 0.9
- tile_lists: int32 [512, 8], P('slab'), may hold values from 0 to 79, as said below
- tile_counts: int32 [512], P('slab'), may hold values from 1 to 8, as said below
- slab_fill: int32 [32], P('slab'), may hold values from 1921 to 2048
Outputs:
- born_radii: float32 [65536], P('slab')
- energy: float32 [65536], P('slab')
- total: float32 [], replicated
Inputs may be any that keep to these rules, and one draw needn't show every extreme that they name: `coords`: x and y lie within 18 of the fibre axis; z of atoms of slab s lies in [8 s, 8 s + 8]. `tile_lists`: entry 0 of tile g's list is its own tile, 32 + g % 16; the entries of a row are distinct; listed tiles lie in slabs that exist (the fibre does not close) and within 32 window tiles of the own tile. `tile_counts`: every slab has a tile whose count is 8.
All inputs are finite; a program needn't handle non-finite values.
Results may differ from a plain program's by a relative error of at most 0.0003.
Values sent between devices are 32-bit elements; how exact they have to be, the bound alone decides.
A program may use at most 64 MiB of HBM per device.

v0:
```python
import jax
import jax.numpy as jnp
from jax import lax
from jax.sharding import PartitionSpec as P

OFFSET = 0.09
SOFTEN = 1.0
group_tiles = 4


def passed_along(value, axis, steps):
    count = lax.axis_size(axis)
    pairs = [(source, (source + steps) % count) for source in range(count)]
    return lax.ppermute(value, axis, pairs)


def pair_geometry(own_atoms, partner_atoms, list_block, count_block, first_block):
    squared = jnp.zeros((own_atoms.shape[1], 128, partner_atoms.shape[2], 128), jnp.float32)
    for component in range(3):
        offsets = own_atoms[component][:, :, None, None] - partner_atoms[component][:, None, :, :]
        squared = squared + offsets * offsets
    slot_ids = jnp.arange(partner_atoms.shape[2], dtype=jnp.int32)
    used_slot = (slot_ids[None, :] < count_block[:, None])[:, None, :, None]
    partner_mask = (
        used_slot & (partner_atoms[6] > 0.5)[:, None, :, :] & (own_atoms[6] > 0.5)[:, :, None, None]
    )
    lanes = jnp.arange(128, dtype=jnp.int32)
    own_ids = first_block[:, None] * 128 + lanes[None, :]
    partner_ids = list_block[:, :, None] * 128 + lanes[None, None, :]
    distinct = own_ids[:, :, None, None] != partner_ids[:, None, :, :]
    return (squared, partner_mask, distinct)


def born_block(own_atoms, partner_atoms, list_block, count_block, first_block):
    squared, partner_mask, distinct = pair_geometry(
        own_atoms, partner_atoms, list_block, count_block, first_block
    )
    own_live = own_atoms[6] > 0.5
    radius_own = jnp.where(own_live, own_atoms[4], 1.5)
    radius_partner = jnp.where(partner_atoms[6] > 0.5, partner_atoms[4], 1.5)[:, None, :, :]
    screen_partner = jnp.where(partner_atoms[6] > 0.5, partner_atoms[5], 0.8)[:, None, :, :]
    offset_radius = (radius_own - OFFSET)[:, :, None, None]
    scaled_radius = screen_partner * (radius_partner - OFFSET)
    distance = jnp.sqrt(squared + SOFTEN)
    upper_end = distance + scaled_radius
    lower_end = jnp.maximum(offset_radius, jnp.abs(distance - scaled_radius))
    pair_term = 0.5 * (
        1.0 / lower_end
        - 1.0 / upper_end
        + 0.25
        * (distance - scaled_radius * scaled_radius / distance)
        * (1.0 / (upper_end * upper_end) - 1.0 / (lower_end * lower_end))
        + 0.5 * jnp.log(lower_end / upper_end) / distance
    )
    pair_term = pair_term + jnp.where(
        offset_radius < scaled_radius - distance, 2.0 * (1.0 / offset_radius - 1.0 / lower_end), 0.0
    )
    counted = partner_mask & distinct & (offset_radius < upper_end)
    integral = jnp.sum(jnp.where(counted, pair_term, 0.0), axis=(2, 3))
    inner_radius = radius_own - OFFSET
    psi_value = integral * inner_radius
    bending = jnp.tanh(
        psi_value - 0.8 * psi_value * psi_value + 4.85 * psi_value * psi_value * psi_value
    )
    result = 1.0 / (1.0 / inner_radius - bending / radius_own)
    return jnp.where(own_live, result, 0.0)


def energy_block(
    own_atoms, partner_atoms, radius_own, radius_partner, list_block, count_block, first_block
):
    squared, partner_mask, distinct = pair_geometry(
        own_atoms, partner_atoms, list_block, count_block, first_block
    )
    own_live = own_atoms[6] > 0.5
    born_own = jnp.where(own_live, radius_own, 1.0)[:, :, None, None]
    born_partner = jnp.where(partner_atoms[6] > 0.5, radius_partner, 1.0)[:, None, :, :]
    product = born_own * born_partner
    screened = jnp.sqrt(squared + product * jnp.exp(-squared / (4.0 * product)))
    pair_term = jnp.where(partner_mask, partner_atoms[3][:, None, :, :] / screened, 0.0)
    result = -0.5 * own_atoms[3] * jnp.sum(pair_term, axis=(2, 3))
    return jnp.where(own_live, result, 0.0)


def tile_setup(window, lists, counts):
    width = window.shape[1]
    tiles = width // 640
    blocks = tiles // group_tiles
    tiled = window.reshape(window.shape[0], width // 128, 128)
    own_atoms = (
        tiled[:, 2 * tiles : 3 * tiles]
        .reshape(window.shape[0], blocks, group_tiles, 128)
        .transpose(1, 0, 2, 3)
    )
    list_groups = lists.reshape(blocks, group_tiles, lists.shape[1])
    count_groups = counts.reshape(blocks, group_tiles)
    first_tiles = (2 * tiles + jnp.arange(tiles, dtype=jnp.int32)).reshape(blocks, group_tiles)
    return (tiled, own_atoms, list_groups, count_groups, first_tiles)


def slab_born(window, lists, counts):
    tiled, own_atoms, list_groups, count_groups, first_tiles = tile_setup(window, lists, counts)

    def one_block(inputs):
        own_block, list_block, count_block, first_block = inputs
        partner_atoms = jnp.take(tiled, list_block, axis=1)
        return born_block(own_block, partner_atoms, list_block, count_block, first_block)

    result = lax.map(one_block, (own_atoms, list_groups, count_groups, first_tiles))
    return result.reshape(-1)


def slab_energy(window, radius_window, lists, counts):
    tiled, own_atoms, list_groups, count_groups, first_tiles = tile_setup(window, lists, counts)
    radius_tiled = radius_window.reshape(-1, 128)
    tiles = radius_tiled.shape[0] // 5
    radius_groups = radius_tiled[2 * tiles : 3 * tiles].reshape(-1, group_tiles, 128)

    def one_block(inputs):
        own_block, radius_block, list_block, count_block, first_block = inputs
        partner_atoms = jnp.take(tiled, list_block, axis=1)
        partner_radii = jnp.take(radius_tiled, list_block, axis=0)
        return energy_block(
            own_block,
            partner_atoms,
            radius_block,
            partner_radii,
            list_block,
            count_block,
            first_block,
        )

    result = lax.map(one_block, (own_atoms, radius_groups, list_groups, count_groups, first_tiles))
    return result.reshape(-1)


def window_of(values):
    nearby = [passed_along(values, "slab", shift_by) for shift_by in (1, -1)]
    distant = [passed_along(values, "slab", shift_by) for shift_by in (2, -2)]
    return jnp.concatenate([distant[0], nearby[0], values, nearby[1], distant[1]], axis=-1)


def shards(coords, charges, radii, screens, tile_lists, tile_counts, slab_fill):
    atom_count = coords.shape[1]
    live_flag = (jnp.arange(atom_count, dtype=jnp.int32) < slab_fill[0]).astype(jnp.float32)
    packed = jnp.concatenate(
        [coords, charges[None], radii[None], screens[None], live_flag[None]], axis=0
    )
    window = window_of(packed)
    born_radii = slab_born(window, tile_lists, tile_counts)
    radius_window = window_of(born_radii)
    energy = slab_energy(window, radius_window, tile_lists, tile_counts)
    total = lax.psum(jnp.sum(energy), "slab")
    return (born_radii, energy, total)


def solution(mesh):
    placed = (
        P(None, "slab"),
        P("slab"),
        P("slab"),
        P("slab"),
        P("slab", None),
        P("slab"),
        P("slab"),
    )
    return jax.shard_map(
        shards, mesh=mesh, in_specs=placed, out_specs=(P("slab"), P("slab"), P()), check_vma=False
    )
```

profile of v0, /device:TPU:0, one launch (start us, length us, event | category | flops | bytes accessed | tf_op | source)
XLA Modules:
  0.0 155.9 jit_solution(13802337545690486778)
XLA Ops:
  1.3 0.8 concatenate.21
  2.1 3.0 %collective-permute-start = (f32[7,2048]{1,0:T(8,128)S(1)}, f32[7,2048]{1,0:T(8,128)S(1)}, u32[]{:S(2)}, u32[]{:S(2)}) collective-permute-start(f32[7,2048]{1,0:T(8,128)S(1)} %concatenate.21), channel_id=1, source_target_pairs={{0,2},{1,3},{2,4},{3,5},{4,6},{5,7},{6,8},{7,9},{8,10},{9,11},{10,... | collective-permute-start | bytes 172040 | tf_op jit(solution)/shard_map/ppermute | solution.py:14
  5.1 5.3 %collective-permute-start.2 = (f32[7,2048]{1,0:T(8,128)S(1)}, f32[7,2048]{1,0:T(8,128)S(1)}, u32[]{:S(2)}, u32[]{:S(2)}) collective-permute-start(f32[7,2048]{1,0:T(8,128)S(1)} %concatenate.21), channel_id=1, source_target_pairs={{0,31},{1,0},{2,1},{3,2},{4,3},{5,4},{6,5},{7,6},{8,7},{9,8},{10,9... | collective-permute-start | bytes 172040 | tf_op jit(solution)/shard_map/ppermute | solution.py:14
  10.9 0.8 copy.25
  11.7 0.7 reshape.487
  12.5 2.2 %collective-permute-done.3 = f32[7,2048]{1,0:T(8,128)S(1)} collective-permute-done((f32[7,2048]{1,0:T(8,128)S(1)}, f32[7,2048]{1,0:T(8,128)S(1)}, u32[]{:S(2)}, u32[]{:S(2)}) %collective-permute-start.3) | collective-permute-done | bytes 57376 | tf_op jit(solution)/shard_map/ppermute | solution.py:14
  14.8 47.0 %while.23 = (s32[]{:T(128)}, f32[4,4,128]{2,1,0:T(4,128)S(1)}, f32[4,7,4,128]{3,2,1,0:T(4,128)S(1)}, s32[4,4]{1,0:T(4,128)S(1)}, s32[4,4,8]{2,1,0:T(4,128)S(1)},...) while((s32[]{:T(128)}, f32[4,4,128]{2,1,0:T(4,128)S(1)}, ...), condition=%wide.region_2.4_spmd, body=%wide.region_0.3_spmd.sunk | while | flops 23141128 | bytes 918585 | solution.py:109
  14.9 0.6 gather_fusion
  16.1 10.4 %fusion.63 = f32[4,128]{1,0:T(4,128)S(1)} fusion(f32[4,128]{1,0:T(4,128)S(1)} %get-tuple-element.337, f32[4,8,128]{2,1,0:T(8,128)S(1)} %get-tuple-element.345, f32[4,8,128]{2,1,0:T(8,128)S(1)} %get-tuple-element.346, f32[4,8,128]{2,1,0:T(8,128)S(1)} %bitcast.188, f32[4,128]{1,0:T(4,128)S(1)} %get-tuple-element.348, f32[4,8,128]{2,1,0:T(8,128)S(1)} %bitcast.189, ...), kind=kLoop, calls=%fused_computation.16.clone.1 | loop fusion | flops 23068160 | bytes 117248 | tf_op jit(solution)/shard_map/while/body/eval_jaxpr/reduce_sum | solution.py:59
  26.7 0.6 gather_fusion
  27.8 10.4 %fusion.63 = f32[4,128]{1,0:T(4,128)S(1)} fusion(f32[4,128]{1,0:T(4,128)S(1)} %get-tuple-element.337, f32[4,8,128]{2,1,0:T(8,128)S(1)} %get-tuple-element.345, f32[4,8,128]{2,1,0:T(8,128)S(1)} %get-tuple-element.346, f32[4,8,128]{2,1,0:T(8,128)S(1)} %bitcast.188, f32[4,128]{1,0:T(4,128)S(1)} %get-tuple-element.348, f32[4,8,128]{2,1,0:T(8,128)S(1)} %bitcast.189, ...), kind=kLoop, calls=%fused_computation.16.clone.1 | loop fusion | flops 23068160 | bytes 117248 | tf_op jit(solution)/shard_map/while/body/eval_jaxpr/reduce_sum | solution.py:59
  38.4 0.6 gather_fusion
  39.6 10.4 %fusion.63 = f32[4,128]{1,0:T(4,128)S(1)} fusion(f32[4,128]{1,0:T(4,128)S(1)} %get-tuple-element.337, f32[4,8,128]{2,1,0:T(8,128)S(1)} %get-tuple-element.345, f32[4,8,128]{2,1,0:T(8,128)S(1)} %get-tuple-element.346, f32[4,8,128]{2,1,0:T(8,128)S(1)} %bitcast.188, f32[4,128]{1,0:T(4,128)S(1)} %get-tuple-element.348, f32[4,8,128]{2,1,0:T(8,128)S(1)} %bitcast.189, ...), kind=kLoop, calls=%fused_computation.16.clone.1 | loop fusion | flops 23068160 | bytes 117248 | tf_op jit(solution)/shard_map/while/body/eval_jaxpr/reduce_sum | solution.py:59
  50.2 0.6 gather_fusion
  51.3 10.4 %fusion.63 = f32[4,128]{1,0:T(4,128)S(1)} fusion(f32[4,128]{1,0:T(4,128)S(1)} %get-tuple-element.337, f32[4,8,128]{2,1,0:T(8,128)S(1)} %get-tuple-element.345, f32[4,8,128]{2,1,0:T(8,128)S(1)} %get-tuple-element.346, f32[4,8,128]{2,1,0:T(8,128)S(1)} %bitcast.188, f32[4,128]{1,0:T(4,128)S(1)} %get-tuple-element.348, f32[4,8,128]{2,1,0:T(8,128)S(1)} %bitcast.189, ...), kind=kLoop, calls=%fused_computation.16.clone.1 | loop fusion | flops 23068160 | bytes 117248 | tf_op jit(solution)/shard_map/while/body/eval_jaxpr/reduce_sum | solution.py:59
  61.9 5.3 %collective-permute-start.6 = (f32[2048]{0:T(1024)S(1)}, f32[2048]{0:T(1024)S(1)}, u32[]{:S(2)}, u32[]{:S(2)}) collective-permute-start(f32[2048]{0:T(1024)S(1)} %bitcast.194), channel_id=1, source_target_pairs={{0,31},{1,0},{2,1},{3,2},{4,3},{5,4},{6,5},{7,6},{8,7},{9,8},{10,9... | collective-permute-start | bytes 24584 | tf_op jit(solution)/shard_map/ppermute | solution.py:14
  67.3 2.0 %collective-permute-start.7 = (f32[2048]{0:T(1024)S(1)}, f32[2048]{0:T(1024)S(1)}, u32[]{:S(2)}, u32[]{:S(2)}) collective-permute-start(f32[2048]{0:T(1024)S(1)} %bitcast.195), channel_id=1, source_target_pairs={{0,30},{1,31},{2,0},{3,1},{4,2},{5,3},{6,4},{7,5},{8,6},{9,7},{10,... | collective-permute-start | bytes 24584 | tf_op jit(solution)/shard_map/ppermute | solution.py:14
  69.3 1.6 %collective-permute-done.7 = f32[2048]{0:T(1024)S(1)} collective-permute-done((f32[2048]{0:T(1024)S(1)}, f32[2048]{0:T(1024)S(1)}, u32[]{:S(2)}, u32[]{:S(2)}) %collective-permute-start.7) | collective-permute-done | bytes 8224 | tf_op jit(solution)/shard_map/ppermute | solution.py:14
  70.9 44.1 %while.24 = (s32[]{:T(128)}, f32[4,4,128]{2,1,0:T(4,128)S(1)}, f32[4,7,4,128]{3,2,1,0:T(4,128)S(1)}, s32[4,4]{1,0:T(4,128)S(1)}, s32[4,4,8]{2,1,0:T(4,128)S(1)},...) while((s32[]{:T(128)}, f32[4,4,128]{2,1,0:T(4,128)S(1)}, ...), condition=%wide.region_5.7_spmd, body=%wide.region_3.6_spmd.sunk | while | flops 9486662 | bytes 816557 | solution.py:133
  71.0 0.6 gather_fusion.1
  72.0 0.6 gather_fusion.2
  72.7 9.3 %select_reduce_fusion.2 = f32[4,128]{1,0:T(4,128)S(1)} fusion(f32[4,8,128]{2,1,0:T(8,128)S(1)} %fusion.66, f32[4,128]{1,0:T(4,128)S(1)} %get-tuple-element.368, f32[4,8,128]{2,1,0:T(8,128)S(1)} %get-tuple-element.369, f32[4,128]{1,0:T(4,128)S(1)} %get-tuple-element.370, f32[4,8,128]{2,1,0:T(8,128)S(1)} %get-tuple-element.371, ...), kind=kLoop, calls=%fused_computation.63.clone.1 | loop fusion | flops 9436672 | bytes 96768 | tf_op jit(solution)/shard_map/while/body/eval_jaxpr/reduce_sum | solution.py:81
  82.1 0.6 gather_fusion.1
  83.0 0.6 gather_fusion.2
  83.7 9.3 %select_reduce_fusion.2 = f32[4,128]{1,0:T(4,128)S(1)} fusion(f32[4,8,128]{2,1,0:T(8,128)S(1)} %fusion.66, f32[4,128]{1,0:T(4,128)S(1)} %get-tuple-element.368, f32[4,8,128]{2,1,0:T(8,128)S(1)} %get-tuple-element.369, f32[4,128]{1,0:T(4,128)S(1)} %get-tuple-element.370, f32[4,8,128]{2,1,0:T(8,128)S(1)} %get-tuple-element.371, ...), kind=kLoop, calls=%fused_computation.63.clone.1 | loop fusion | flops 9436672 | bytes 96768 | tf_op jit(solution)/shard_map/while/body/eval_jaxpr/reduce_sum | solution.py:81
  93.1 0.6 gather_fusion.1
  94.7 9.3 %select_reduce_fusion.2 = f32[4,128]{1,0:T(4,128)S(1)} fusion(f32[4,8,128]{2,1,0:T(8,128)S(1)} %fusion.66, f32[4,128]{1,0:T(4,128)S(1)} %get-tuple-element.368, f32[4,8,128]{2,1,0:T(8,128)S(1)} %get-tuple-element.369, f32[4,128]{1,0:T(4,128)S(1)} %get-tuple-element.370, f32[4,8,128]{2,1,0:T(8,128)S(1)} %get-tuple-element.371, ...), kind=kLoop, calls=%fused_computation.63.clone.1 | loop fusion | flops 9436672 | bytes 96768 | tf_op jit(solution)/shard_map/while/body/eval_jaxpr/reduce_sum | solution.py:81
  104.1 0.6 gather_fusion.1
  105.1 0.6 gather_fusion.2
  105.8 9.3 %select_reduce_fusion.2 = f32[4,128]{1,0:T(4,128)S(1)} fusion(f32[4,8,128]{2,1,0:T(8,128)S(1)} %fusion.66, f32[4,128]{1,0:T(4,128)S(1)} %get-tuple-element.368, f32[4,8,128]{2,1,0:T(8,128)S(1)} %get-tuple-element.369, f32[4,128]{1,0:T(4,128)S(1)} %get-tuple-element.370, f32[4,8,128]{2,1,0:T(8,128)S(1)} %get-tuple-element.371, ...), kind=kLoop, calls=%fused_computation.63.clone.1 | loop fusion | flops 9436672 | bytes 96768 | tf_op jit(solution)/shard_map/while/body/eval_jaxpr/reduce_sum | solution.py:81
  115.1 0.6 reduce_sum.35
  115.7 40.2 %psum.7 = f32[]{:T(128)} all-reduce(f32[]{:T(128)} %reduce_sum.35), channel_id=1, replica_groups=mesh['slab'=32] {'slab'}, use_global_device_ids=true, to_apply=%region_7.9 | all-reduce | flops 1 | bytes 8 | tf_op jit(solution)/shard_map/psum | solution.py:153
  (151 shorter events, 6.2 us)
Async XLA Ops:
  2.1 10.3 %collective-permute-start = (f32[7,2048]{1,0:T(8,128)S(1)}, f32[7,2048]{1,0:T(8,128)S(1)}, u32[]{:S(2)}, u32[]{:S(2)}) collective-permute-start(f32[7,2048]{1,0:T(8,128)S(1)} %concatenate.21), channel_id=1, source_target_pairs={{0,2},{1,3},{2,4},{3,5},{4,6},{5,7},{6,8},{7,9},{8,10},{9,11},{10,... | collective-permute-start | bytes 172040 | tf_op jit(solution)/shard_map/ppermute | solution.py:14
  5.1 7.3 %collective-permute-start.1 = (f32[7,2048]{1,0:T(8,128)S(1)}, f32[7,2048]{1,0:T(8,128)S(1)}, u32[]{:S(2)}, u32[]{:S(2)}) collective-permute-start(f32[7,2048]{1,0:T(8,128)S(1)} %concatenate.21), channel_id=1, source_target_pairs={{0,1},{1,2},{2,3},{3,4},{4,5},{5,6},{6,7},{7,8},{8,9},{9,10},{10,1... | collective-permute-start | bytes 172040 | tf_op jit(solution)/shard_map/ppermute | solution.py:14
  5.1 7.4 %collective-permute-start.2 = (f32[7,2048]{1,0:T(8,128)S(1)}, f32[7,2048]{1,0:T(8,128)S(1)}, u32[]{:S(2)}, u32[]{:S(2)}) collective-permute-start(f32[7,2048]{1,0:T(8,128)S(1)} %concatenate.21), channel_id=1, source_target_pairs={{0,31},{1,0},{2,1},{3,2},{4,3},{5,4},{6,5},{7,6},{8,7},{9,8},{10,9... | collective-permute-start | bytes 172040 | tf_op jit(solution)/shard_map/ppermute | solution.py:14
  10.5 4.3 %collective-permute-start.3 = (f32[7,2048]{1,0:T(8,128)S(1)}, f32[7,2048]{1,0:T(8,128)S(1)}, u32[]{:S(2)}, u32[]{:S(2)}) collective-permute-start(f32[7,2048]{1,0:T(8,128)S(1)} %concatenate.21), channel_id=1, source_target_pairs={{0,30},{1,31},{2,0},{3,1},{4,2},{5,3},{6,4},{7,5},{8,6},{9,7},{10,... | collective-permute-start | bytes 172040 | tf_op jit(solution)/shard_map/ppermute | solution.py:14
  61.8 7.4 %collective-permute-start.4 = (f32[2048]{0:T(1024)S(1)}, f32[2048]{0:T(1024)S(1)}, u32[]{:S(2)}, u32[]{:S(2)}) collective-permute-start(f32[2048]{0:T(1024)S(1)} %bitcast.192), channel_id=1, source_target_pairs={{0,2},{1,3},{2,4},{3,5},{4,6},{5,7},{6,8},{7,9},{8,10},{9,11},{10,... | collective-permute-start | bytes 24584 | tf_op jit(solution)/shard_map/ppermute | solution.py:14
  61.9 7.4 %collective-permute-start.5 = (f32[2048]{0:T(1024)S(1)}, f32[2048]{0:T(1024)S(1)}, u32[]{:S(2)}, u32[]{:S(2)}) collective-permute-start(f32[2048]{0:T(1024)S(1)} %bitcast.193), channel_id=1, source_target_pairs={{0,1},{1,2},{2,3},{3,4},{4,5},{5,6},{6,7},{7,8},{8,9},{9,10},{10,1... | collective-permute-start | bytes 24584 | tf_op jit(solution)/shard_map/ppermute | solution.py:14
  61.9 7.3 %collective-permute-start.6 = (f32[2048]{0:T(1024)S(1)}, f32[2048]{0:T(1024)S(1)}, u32[]{:S(2)}, u32[]{:S(2)}) collective-permute-start(f32[2048]{0:T(1024)S(1)} %bitcast.194), channel_id=1, source_target_pairs={{0,31},{1,0},{2,1},{3,2},{4,3},{5,4},{6,5},{7,6},{8,7},{9,8},{10,9... | collective-permute-start | bytes 24584 | tf_op jit(solution)/shard_map/ppermute | solution.py:14
  67.3 3.7 %collective-permute-start.7 = (f32[2048]{0:T(1024)S(1)}, f32[2048]{0:T(1024)S(1)}, u32[]{:S(2)}, u32[]{:S(2)}) collective-permute-start(f32[2048]{0:T(1024)S(1)} %bitcast.195), channel_id=1, source_target_pairs={{0,30},{1,31},{2,0},{3,1},{4,2},{5,3},{6,4},{7,5},{8,6},{9,7},{10,... | collective-permute-start | bytes 24584 | tf_op jit(solution)/shard_map/ppermute | solution.py:14
  115.1 40.8 %copy-start = (f32[4,4,128]{2,1,0:T(4,128)}, f32[4,4,128]{2,1,0:T(4,128)S(1)}, u32[]{:S(2)}) copy-start(f32[4,4,128]{2,1,0:T(4,128)S(1)} %get-tuple-element.470) | copy-start | bytes 24580
  115.1 40.8 %copy-start.1 = (f32[4,4,128]{2,1,0:T(4,128)}, f32[4,4,128]{2,1,0:T(4,128)S(1)}, u32[]{:S(2)}) copy-start(f32[4,4,128]{2,1,0:T(4,128)S(1)} %get-tuple-element.156) | copy-start | bytes 24580
where the time goes:
time: 156 us
  other arithmetic  82.8 us (53%)
  blocking collectives  40.2 us (26%)
  starting transfers between devices  16.2 us (10%)
  local copies, waits for them, and re-layouts  10.9 us (7%)
  waiting for transfers between devices  3.89 us (2%)
    reduce_sum x4, other arithmetic, born_block(): integral = jnp.sum(jnp.where(counted, pair_term, 0.0), axis=(2, 3))  41.8 us
    psum x1, blocking collectives, shards(): total = lax.psum(jnp.sum(energy), 'slab')  40.2 us
    reduce_sum x4, other arithmetic, energy_block(): result = -0.5 * own_atoms[3] * jnp.sum(pair_term, axis=(2, 3))  37 us
    ppermute x8, starting transfers between devices, passed_along(): return lax.ppermute(value, axis, pairs)  16.2 us
    gather x8, local copies, waits for them, and re-layouts, one_block(): partner_atoms = jnp.take(tiled, list_block, axis=1)  4.68 us
    ppermute x8, waiting for transfers between devices, passed_along(): return lax.ppermute(value, axis, pairs)  3.89 us
  transfers between devices with their start and end apart: 8, of which 2 were waited for; matrix products, arithmetic and copies ran while one was open for 1% of the time, Pallas kernels for 0%

commit v1 on v0

v1 whole, which is shorter than its diff:
```python
import functools

import jax
import jax.numpy as jnp
from jax import lax
from jax.experimental import pallas as pl
from jax.experimental.pallas import tpu as pltpu
from jax.sharding import PartitionSpec as P

OFFSET = 0.09
SOFTEN = 1.0
LOG2E = 1.4426950408889634
MESH = pl.DeviceIdType.MESH
SHIFTS = (1, -1, 2, -2)
LANES = 128
ROWS = 8


def squared_distance(own, partner):
    dx = own[0] - partner[0]
    dy = own[1] - partner[1]
    dz = own[2] - partner[2]
    return dx * dx + dy * dy + dz * dz


def born_parts(squared, offset_own, scaled, diagonal=None):
    soft = squared + SOFTEN
    inverse = lax.rsqrt(soft)
    distance = soft * inverse
    upper = distance + scaled
    reach = distance - scaled
    inner = jnp.maximum(offset_own, scaled - distance)
    lower = jnp.minimum(jnp.maximum(inner, reach), upper)
    both = pl.reciprocal(upper * lower, approx=True)
    over_lower = upper * both
    over_upper = lower * both
    apart = over_lower - over_upper
    bend = distance - scaled * scaled * inverse
    first = apart * (4.0 - bend * (over_lower + over_upper))
    second = inverse * jnp.log(lower * over_upper)
    third = (inner - offset_own) * over_lower
    if diagonal is not None:
        first = jnp.where(diagonal, 0.0, first)
        second = jnp.where(diagonal, 0.0, second)
        third = jnp.where(diagonal, 0.0, third)
    return first, second, third


def energy_part(squared, born_own, rate_own, born_partner, over_partner, charge_partner):
    spread = jnp.exp2(squared * (rate_own * over_partner))
    return charge_partner * lax.rsqrt(squared + (born_own * born_partner) * spread)


def kernel(
    count,
    lists,
    counts,
    fill,
    coords,
    charges,
    radii,
    screens,
    born_out,
    energy_out,
    total_out,
    window,
    born_window,
    total_window,
    columns,
    born_columns,
    partners,
    sums,
    result,
    window_send,
    window_recv,
    born_send,
    born_recv,
    total_send,
    total_recv,
):
    me = lax.axis_index("slab")
    tiles = charges.shape[0]
    width = lists.shape[1]
    steps = LANES // ROWS

    barrier = pltpu.get_barrier_semaphore()

    def greet(step, carry):
        pl.semaphore_signal(
            barrier, inc=1, device_id=(lax.rem(me + step, count),), device_id_type=MESH
        )
        return carry

    lax.fori_loop(1, count, greet, 0)

    slots = lax.broadcasted_iota(jnp.int32, (tiles, LANES), 0) * LANES
    slots = slots + lax.broadcasted_iota(jnp.int32, (tiles, LANES), 1)
    live = slots < fill[0]
    offset_own = jnp.where(live, radii[...] - OFFSET, 1.5 - OFFSET)
    home = pl.ds(2 * tiles, tiles)
    for component in range(3):
        for tile in range(tiles):
            window[component, 2 * tiles + tile : 2 * tiles + tile + 1, :] = coords[
                component : component + 1, tile * LANES : (tile + 1) * LANES
            ]
    window[3, home, :] = jnp.where(live, charges[...], 0.0)
    window[4, home, :] = jnp.where(live, screens[...] * (radii[...] - OFFSET), 0.0)
    result[...] = offset_own

    def there(shift):
        return jnp.logical_and(me + shift >= 0, me + shift < count)

    def send(buffer, sems_out, sems_in, place, shift):
        def view(spot):
            rows = pl.ds(spot * tiles, tiles)
            return buffer.at[:, rows, :] if len(buffer.shape) == 3 else buffer.at[rows, :]

        return pltpu.make_async_remote_copy(
            src_ref=view(2),
            dst_ref=view(2 - shift),
            send_sem=sems_out.at[place],
            recv_sem=sems_in.at[place],
            device_id=(me + shift,),
            device_id_type=MESH,
        )

    def send_all(buffer, sems_out, sems_in):
        for place, shift in enumerate(SHIFTS):
            copy = send(buffer, sems_out, sems_in, place, shift)
            pl.when(there(shift))(copy.start)

    def wait_all(buffer, sems_out, sems_in):
        for place, shift in enumerate(SHIFTS):
            copy = send(buffer, sems_out, sems_in, place, shift)
            pl.when(there(shift))(copy.wait_send)
            pl.when(there(-shift))(copy.wait_recv)

    for shift in SHIFTS:

        @pl.when(jnp.logical_not(there(-shift)))
        def _():
            rows = pl.ds((2 - shift) * tiles, tiles)
            window[:, rows, :] = jnp.zeros((5, tiles, LANES), jnp.float32)
            born_window[rows, :] = jnp.ones((tiles, LANES), jnp.float32)

    pl.semaphore_wait(barrier, count - 1)
    send_all(window, window_send, window_recv)

    def diagonal_of(row):
        own_slot = lax.broadcasted_iota(jnp.int32, (ROWS, LANES), 0) + row
        return own_slot == lax.broadcasted_iota(jnp.int32, (ROWS, LANES), 1)

    def row_of(buffer, index):
        return jnp.broadcast_to(buffer[pl.ds(index, 1), :], (ROWS, LANES))

    def spread_columns(rows):
        return [jnp.broadcast_to(row, (LANES, LANES)).T for row in rows]

    def born_near(tile, carry):
        own_rows = [window[c, pl.ds(2 * tiles + tile, 1), :] for c in range(3)]
        own_rows.append(result[pl.ds(tile, 1), :])
        for place, block in enumerate(spread_columns(own_rows)):
            columns[tile, place] = block
        partner = [row_of(window.at[c], 2 * tiles + tile) for c in (0, 1, 2, 4)]
        for step in range(steps):
            rows = pl.ds(step * ROWS, ROWS)
            own = [columns[tile, c, rows, :] for c in range(4)]
            terms = born_parts(
                squared_distance(own, partner), own[3], partner[3], diagonal_of(step * ROWS)
            )
            for place, term in enumerate(terms):
                sums[tile, place, rows, :] = term
        return carry

    lax.fori_loop(0, tiles, born_near, 0)
    wait_all(window, window_send, window_recv)

    def gather_partner(tile, entry):
        index = lists[tile, entry]
        used = entry < counts[tile]
        for place in range(5):
            row = row_of(window.at[place], index)
            partners[entry, place] = jnp.where(used, row, 0.0)
        return index, used

    def born_far(tile, carry):
        for entry in range(1, width):
            gather_partner(tile, entry)

        def one_step(step, inner):
            rows = pl.ds(pl.multiple_of(step * ROWS, ROWS), ROWS)
            own = [columns[tile, c, rows, :] for c in range(4)]
            totals = [sums[tile, c, rows, :] for c in range(3)]
            for entry in range(1, width):
                partner = [partners[entry, c] for c in (0, 1, 2, 4)]
                terms = born_parts(squared_distance(own, partner), own[3], partner[3])
                totals = [old + term for old, term in zip(totals, terms)]
            sums[tile, 0, rows, :] = 0.125 * totals[0] + 0.25 * totals[1] + 2.0 / own[3] * totals[2]
            return inner

        lax.fori_loop(0, steps, one_step, 0, unroll=2)
        born_out[pl.ds(tile, 1), :] = jnp.sum(sums[tile, 0].T, axis=0, keepdims=True)
        return carry

    lax.fori_loop(0, tiles, born_far, 0)

    radius_own = jnp.where(live, radii[...], 1.5)
    psi = born_out[...] * offset_own
    bending = jnp.tanh(psi - 0.8 * psi * psi + 4.85 * psi * psi * psi)
    born = 1.0 / (1.0 / offset_own - bending / radius_own)
    born_out[...] = jnp.where(live, born, 0.0)
    born_window[home, :] = jnp.where(live, born, 1.0)
    send_all(born_window, born_send, born_recv)

    def energy_near(tile, carry):
        own_born = born_window[pl.ds(2 * tiles + tile, 1), :]
        blocks = spread_columns([own_born, (-0.25 * LOG2E) / own_born])
        for place, block in enumerate(blocks):
            born_columns[tile, place] = block
        partner = [row_of(window.at[c], 2 * tiles + tile) for c in range(4)]
        partner_born = row_of(born_window, 2 * tiles + tile)
        over_partner = 1.0 / partner_born
        for step in range(steps):
            rows = pl.ds(step * ROWS, ROWS)
            own = [columns[tile, c, rows, :] for c in range(3)]
            sums[tile, 0, rows, :] = energy_part(
                squared_distance(own, partner),
                born_columns[tile, 0, rows, :],
                born_columns[tile, 1, rows, :],
                partner_born,
                over_partner,
                partner[3],
            )
        return carry

    lax.fori_loop(0, tiles, energy_near, 0)
    wait_all(born_window, born_send, born_recv)

    def energy_far(tile, carry):
        for entry in range(1, width):
            index, used = gather_partner(tile, entry)
            row = jnp.where(used, row_of(born_window, index), 1.0)
            partners[entry, 4] = row
            partners[entry, 5] = 1.0 / row

        def one_step(step, inner):
            rows = pl.ds(pl.multiple_of(step * ROWS, ROWS), ROWS)
            own = [columns[tile, c, rows, :] for c in range(3)]
            own_born = [born_columns[tile, c, rows, :] for c in range(2)]
            total = sums[tile, 0, rows, :]
            for entry in range(1, width):
                partner = [partners[entry, c] for c in range(6)]
                total = total + energy_part(
                    squared_distance(own, partner), *own_born, partner[4], partner[5], partner[3]
                )
            sums[tile, 0, rows, :] = total
            return inner

        lax.fori_loop(0, steps, one_step, 0, unroll=2)
        result[pl.ds(tile, 1), :] = jnp.sum(sums[tile, 0].T, axis=0, keepdims=True)
        return carry

    lax.fori_loop(0, tiles, energy_far, 0)

    energy = -0.5 * window[3, home, :] * result[...]
    energy_out[...] = energy
    total_window[pl.ds(me, 1), :] = jnp.sum(energy, axis=0, keepdims=True)

    def total_copy(step):
        mine = total_window.at[pl.ds(me, 1), :]
        return pltpu.make_async_remote_copy(
            src_ref=mine,
            dst_ref=mine,
            send_sem=total_send.at[step],
            recv_sem=total_recv.at[step],
            device_id=(lax.rem(me + step, count),),
            device_id_type=MESH,
        )

    def total_start(step, carry):
        total_copy(step).start()
        return carry

    def total_wait(step, carry):
        total_copy(step).wait_recv()
        return carry

    def total_sent(step, carry):
        total_copy(step).wait_send()
        return carry

    lax.fori_loop(1, count, total_start, 0)
    lax.fori_loop(1, count, total_wait, 0)
    total_out[0, 0] = jnp.sum(total_window[...])
    lax.fori_loop(1, count, total_sent, 0)


def solution(mesh):
    count = mesh.shape["slab"]

    def shards(coords, charges, radii, screens, tile_lists, tile_counts, slab_fill):
        tiles = charges.shape[0] // LANES
        width = tile_lists.shape[1]
        block = jax.ShapeDtypeStruct((tiles, LANES), jnp.float32)
        smem = pl.BlockSpec(memory_space=pltpu.SMEM)
        vmem = pl.BlockSpec(memory_space=pltpu.VMEM)
        born, energy, total = pl.pallas_call(
            functools.partial(kernel, count),
            out_shape=(block, block, jax.ShapeDtypeStruct((1, 1), jnp.float32)),
            in_specs=[smem] * 3 + [vmem] * 4,
            out_specs=(vmem, vmem, smem),
            scratch_shapes=[
                pltpu.VMEM((5, 5 * tiles, LANES), jnp.float32),
                pltpu.VMEM((5 * tiles, LANES), jnp.float32),
                pltpu.VMEM((count, LANES), jnp.float32),
                pltpu.VMEM((tiles, 4, LANES, LANES), jnp.float32),
                pltpu.VMEM((tiles, 2, LANES, LANES), jnp.float32),
                pltpu.VMEM((width, 6, ROWS, LANES), jnp.float32),
                pltpu.VMEM((tiles, 3, LANES, LANES), jnp.float32),
                pltpu.VMEM((tiles, LANES), jnp.float32),
                pltpu.SemaphoreType.DMA((len(SHIFTS),)),
                pltpu.SemaphoreType.DMA((len(SHIFTS),)),
                pltpu.SemaphoreType.DMA((len(SHIFTS),)),
                pltpu.SemaphoreType.DMA((len(SHIFTS),)),
                pltpu.SemaphoreType.DMA((count,)),
                pltpu.SemaphoreType.DMA((count,)),
            ],
            compiler_params=pltpu.CompilerParams(
                collective_id=0, has_side_effects=True, vmem_limit_bytes=40 * 1024 * 1024
            ),
        )(
            tile_lists,
            tile_counts,
            slab_fill,
            coords,
            charges.reshape(tiles, LANES),
            radii.reshape(tiles, LANES),
            screens.reshape(tiles, LANES),
        )
        return born.reshape(-1), energy.reshape(-1), total.reshape(())

    placed = (
        P(None, "slab"),
        P("slab"),
        P("slab"),
        P("slab"),
        P("slab", None),
        P("slab"),
        P("slab"),
    )
    return jax.shard_map(
        shards, mesh=mesh, in_specs=placed, out_specs=(P("slab"), P("slab"), P()), check_vma=False
    )
```

time: 156 us -> 49.1 us (0.31)
  other arithmetic: 82.8 us -> 0 us
  Pallas kernels: 0 us -> 42.4 us
  blocking collectives: 40.2 us -> 0 us
  starting transfers between devices: 16.2 us -> 0 us
  local copies, waits for them, and re-layouts: 10.9 us -> 3.44 us
  waiting for transfers between devices: 3.89 us -> 0 us
  between operations: 1.42 us -> 3.01 us
    reduce_sum x9 -> x0, other arithmetic: 79.4 us -> none  [the longest x4 41.8 us: born_block(): integral = jnp.sum(jnp.where(counted, pair_term, 0.0), axis=(2, 3))]
    pallas_call x0 -> x1, Pallas kernels: none -> 42.4 us  [shards(): pl.pallas_call(functools.partial(kernel, count), out_shape=(block, block,...]
    psum x1 -> x0, blocking collectives: 40.2 us -> none  [shards(): total = lax.psum(jnp.sum(energy), 'slab')]
    ppermute x8 -> x0, starting transfers between devices: 16.2 us -> none  [passed_along(): return lax.ppermute(value, axis, pairs)]
    gather x12 -> x0, local copies, waits for them, and re-layouts: 6.98 us -> none  [the longest x8 4.68 us: one_block(): partner_atoms = jnp.take(tiled, list_block, axis=1)]
    ppermute x8 -> x0, waiting for transfers between devices: 3.89 us -> none  [passed_along(): return lax.ppermute(value, axis, pairs)]
    unnamed x13, local copies, waits for them, and re-layouts: 0.81 us -> 3.44 us
  transfers between devices with their start and end apart: 8 -> 0, of which waited for: 2 -> 0; matrix products, arithmetic and copies ran while one was open for 1% -> 0% of each run, Pallas kernels for 0% -> 0%
where the time goes in v1:
time: 49.1 us; the launch traced here: 48.8 us
  Pallas kernels  42.4 us (86%)
  local copies, waits for them, and re-layouts  3.44 us (7%)
  between operations  3.01 us (6%)
    pallas_call x1, Pallas kernels, shards(): pl.pallas_call(functools.partial(kernel, count), out_shape=(block, block,...  42.4 us
    unnamed x13, local copies, waits for them, and re-layouts  3.44 us

profile of v1, /device:TPU:0, one launch (start us, length us, event | category | flops | bytes accessed | tf_op | source)
XLA Modules:
  0.0 48.8 jit_solution(6688620638595498699)
XLA Ops:
  1.3 0.0 copy-start.2
  1.3 0.0 copy-start.1
  1.3 0.0 copy-start.4
  1.3 0.8 %copy.10.lists = s32[16,8]{1,0:T(8,128)S(1)} copy(s32[16,8]{0,1:T(8,128)} %param.11) | data formatting | bytes 1024 | tf_op args[4]
  2.1 0.0 copy-done.2
  2.1 0.0 copy-done.1
  2.1 0.0 copy-done.4
  2.1 0.0 copy-start
  2.1 0.7 %copy-done = f32[3,2048]{1,0:T(4,128)S(1)} copy-done((f32[3,2048]{1,0:T(4,128)S(1)}, f32[3,2048]{1,0:T(4,128)}, u32[]{:S(2)}) %copy-start) | copy-done | bytes 24600
  2.9 0.0 copy-start.3
  2.9 0.7 %copy-done.3 = f32[2048]{0:T(1024)S(1)} copy-done((f32[2048]{0:T(1024)S(1)}, f32[2048]{0:T(1024)}, u32[]{:S(2)}) %copy-start.3) | copy-done | bytes 8216
  3.6 42.4 %shard_map.94 = (f32[16,128]{1,0:T(8,128)S(1)}, f32[16,128]{1,0:T(8,128)S(1)}, f32[1,1]{1,0:T(1,128)}) custom-call(s32[16,8]{1,0:T(8,128)S(1)} %copy.10.lists, s32[16]{0:T(128)S(1)} %copy-done.4, s32[1]{0:T(128)S(6)} %copy.14.fill, f32[3,2048]{1,0:T(4,128)S(1)} %copy-done, f32[16,128]{1,0:T(8,128)S(1)} %bitcast.8, f32[16,128]{1,0:T(8,128)S(1)} %bitcast.9, ...), custom_call_target="tpu_custom_call" | custom-call | tf_op jit(solution)/shard_map/pallas_call | solution.py:307
  45.9 0.6 %copy.15 = f32[2048]{0:T(1024)} copy(f32[2048]{0:T(1024)S(1)} %bitcast.7) | data formatting | bytes 16384
  46.5 0.6 %copy.16 = f32[2048]{0:T(1024)} copy(f32[2048]{0:T(1024)S(1)} %bitcast.6) | data formatting | bytes 16384
Async XLA Ops:
  1.3 0.8 %copy-start.2 = (f32[2048]{0:T(1024)S(1)}, f32[2048]{0:T(1024)}, u32[]{:S(2)}) copy-start(f32[2048]{0:T(1024)} %param.9) | copy-start | bytes 24580
  1.3 0.8 %copy-start.1 = (f32[2048]{0:T(1024)S(1)}, f32[2048]{0:T(1024)}, u32[]{:S(2)}) copy-start(f32[2048]{0:T(1024)} %param.8) | copy-start | bytes 24580
  1.3 0.8 %copy-start.4 = (s32[16]{0:T(128)S(1)}, s32[16]{0:T(128)}, u32[]{:S(2)}) copy-start(s32[16]{0:T(128)} %counts.1) | copy-start | bytes 196
  2.1 0.8 %copy-start = (f32[3,2048]{1,0:T(4,128)S(1)}, f32[3,2048]{1,0:T(4,128)}, u32[]{:S(2)}) copy-start(f32[3,2048]{1,0:T(4,128)} %coords.1) | copy-start | bytes 73732
  2.9 0.7 %copy-start.3 = (f32[2048]{0:T(1024)S(1)}, f32[2048]{0:T(1024)}, u32[]{:S(2)}) copy-start(f32[2048]{0:T(1024)} %param.10) | copy-start | bytes 24580

commit v2 on v1

--- a/solution.py
+++ b/solution.py
@@ -46,13 +46,23 @@
     return first, second, third
 
 
-def energy_part(squared, born_own, rate_own, born_partner, over_partner, charge_partner):
-    spread = jnp.exp2(squared * (rate_own * over_partner))
-    return charge_partner * lax.rsqrt(squared + (born_own * born_partner) * spread)
+def energy_part(squared, own_over, partner_over, partner_charge):
+    scaled = squared * (own_over * partner_over)
+    return partner_charge * lax.rsqrt(scaled + jnp.exp2(scaled * (-0.25 * LOG2E)))
 
 
 def kernel(
     count,
+    lists_in,
+    counts_in,
+    fill_in,
+    coords_in,
+    charges_in,
+    radii_in,
+    screens_in,
+    born_out,
+    energy_out,
+    total_out,
     lists,
     counts,
     fill,
@@ -60,17 +70,18 @@
     charges,
     radii,
     screens,
-    born_out,
-    energy_out,
-    total_out,
     window,
     born_window,
+    over_window,
+    charge_window,
     total_window,
     columns,
     born_columns,
     partners,
     sums,
-    result,
+    distances,
+    collected,
+    load_sems,
     window_send,
     window_recv,
     born_send,
@@ -80,8 +91,25 @@
 ):
     me = lax.axis_index("slab")
     tiles = charges.shape[0]
-    width = lists.shape[1]
+    width = lists.shape[0]
     steps = LANES // ROWS
+
+    loads = [
+        pltpu.make_async_copy(source, target, load_sems.at[place])
+        for place, (source, target) in enumerate(
+            (
+                (fill_in, fill),
+                (radii_in, radii),
+                (screens_in, screens),
+                (charges_in, charges),
+                (coords_in, coords),
+                (lists_in, lists),
+                (counts_in, counts),
+            )
+        )
+    ]
+    for load in loads:
+        load.start()
 
     barrier = pltpu.get_barrier_semaphore()
 
@@ -92,6 +120,8 @@
         return carry
 
     lax.fori_loop(1, count, greet, 0)
+    for load in loads:
+        load.wait()
 
     slots = lax.broadcasted_iota(jnp.int32, (tiles, LANES), 0) * LANES
     slots = slots + lax.broadcasted_iota(jnp.int32, (tiles, LANES), 1)
@@ -105,7 +135,6 @@
             ]
     window[3, home, :] = jnp.where(live, charges[...], 0.0)
     window[4, home, :] = jnp.where(live, screens[...] * (radii[...] - OFFSET), 0.0)
-    result[...] = offset_own
 
     def there(shift):
         return jnp.logical_and(me + shift >= 0, me + shift < count)
@@ -153,21 +182,32 @@
     def row_of(buffer, index):
         return jnp.broadcast_to(buffer[pl.ds(index, 1), :], (ROWS, LANES))
 
-    def spread_columns(rows):
-        return [jnp.broadcast_to(row, (LANES, LANES)).T for row in rows]
+    def spread_columns(values, block, place):
+        turned = values.T
+        for tile in range(tiles):
+            block[tile, place] = jnp.broadcast_to(turned[:, tile : tile + 1], (LANES, LANES))
+
+    for component in range(3):
+        spread_columns(window[component, home, :], columns, component)
+    spread_columns(offset_own, columns, 3)
+    collected[...] = jnp.zeros((LANES, LANES), jnp.float32)
+
+    def collect(tile, rows, values):
+        lane = lax.broadcasted_iota(jnp.int32, (ROWS, LANES), 1)
+        row_sums = jnp.sum(values, axis=1, keepdims=True)
+        collected[rows, :] = jnp.where(lane == tile, row_sums, collected[rows, :])
+
+    def collected_rows():
+        return collected[...].T[:tiles, :]
 
     def born_near(tile, carry):
-        own_rows = [window[c, pl.ds(2 * tiles + tile, 1), :] for c in range(3)]
-        own_rows.append(result[pl.ds(tile, 1), :])
-        for place, block in enumerate(spread_columns(own_rows)):
-            columns[tile, place] = block
         partner = [row_of(window.at[c], 2 * tiles + tile) for c in (0, 1, 2, 4)]
         for step in range(steps):
             rows = pl.ds(step * ROWS, ROWS)
             own = [columns[tile, c, rows, :] for c in range(4)]
-            terms = born_parts(
-                squared_distance(own, partner), own[3], partner[3], diagonal_of(step * ROWS)
-            )
+            squared = squared_distance(own, partner)
+            distances[tile, 0, rows, :] = squared
+            terms = born_parts(squared, own[3], partner[3], diagonal_of(step * ROWS))
             for place, term in enumerate(terms):
                 sums[tile, place, rows, :] = term
         return carry
@@ -175,94 +215,85 @@
     lax.fori_loop(0, tiles, born_near, 0)
     wait_all(window, window_send, window_recv)
 
-    def gather_partner(tile, entry):
-        index = lists[tile, entry]
-        used = entry < counts[tile]
-        for place in range(5):
-            row = row_of(window.at[place], index)
-            partners[entry, place] = jnp.where(used, row, 0.0)
-        return index, used
-
     def born_far(tile, carry):
         for entry in range(1, width):
-            gather_partner(tile, entry)
+            index = lists[entry, tile]
+            for place in range(3):
+                partners[entry, place] = row_of(window.at[place], index)
+            partners[entry, 3] = jnp.where(entry < counts[tile], row_of(window.at[4], index), 0.0)
 
         def one_step(step, inner):
             rows = pl.ds(pl.multiple_of(step * ROWS, ROWS), ROWS)
             own = [columns[tile, c, rows, :] for c in range(4)]
             totals = [sums[tile, c, rows, :] for c in range(3)]
             for entry in range(1, width):
-                partner = [partners[entry, c] for c in (0, 1, 2, 4)]
-                terms = born_parts(squared_distance(own, partner), own[3], partner[3])
+                partner = [partners[entry, c] for c in range(4)]
+                squared = squared_distance(own, partner)
+                distances[tile, entry, rows, :] = squared
+                terms = born_parts(squared, own[3], partner[3])
                 totals = [old + term for old, term in zip(totals, terms)]
-            sums[tile, 0, rows, :] = 0.125 * totals[0] + 0.25 * totals[1] + 2.0 / own[3] * totals[2]
+            collect(
+                tile, rows, 0.125 * totals[0] + 0.25 * totals[1] + (2.0 / own[3]) * totals[2]
+            )
             return inner
 
         lax.fori_loop(0, steps, one_step, 0, unroll=2)
-        born_out[pl.ds(tile, 1), :] = jnp.sum(sums[tile, 0].T, axis=0, keepdims=True)
         return carry
 
     lax.fori_loop(0, tiles, born_far, 0)
 
     radius_own = jnp.where(live, radii[...], 1.5)
-    psi = born_out[...] * offset_own
+    psi = collected_rows() * offset_own
     bending = jnp.tanh(psi - 0.8 * psi * psi + 4.85 * psi * psi * psi)
     born = 1.0 / (1.0 / offset_own - bending / radius_own)
     born_out[...] = jnp.where(live, born, 0.0)
     born_window[home, :] = jnp.where(live, born, 1.0)
     send_all(born_window, born_send, born_recv)
 
+    own_over = 1.0 / born_window[home, :]
+    over_window[home, :] = own_over
+    charge_window[home, :] = window[3, home, :] * lax.rsqrt(born_window[home, :])
+    spread_columns(own_over, born_columns, 0)
+
     def energy_near(tile, carry):
-        own_born = born_window[pl.ds(2 * tiles + tile, 1), :]
-        blocks = spread_columns([own_born, (-0.25 * LOG2E) / own_born])
-        for place, block in enumerate(blocks):
-            born_columns[tile, place] = block
-        partner = [row_of(window.at[c], 2 * tiles + tile) for c in range(4)]
-        partner_born = row_of(born_window, 2 * tiles + tile)
-        over_partner = 1.0 / partner_born
+        partner = [row_of(buffer, 2 * tiles + tile) for buffer in (over_window, charge_window)]
         for step in range(steps):
             rows = pl.ds(step * ROWS, ROWS)
-            own = [columns[tile, c, rows, :] for c in range(3)]
             sums[tile, 0, rows, :] = energy_part(
-                squared_distance(own, partner),
-                born_columns[tile, 0, rows, :],
-                born_columns[tile, 1, rows, :],
-                partner_born,
-                over_partner,
-                partner[3],
+                distances[tile, 0, rows, :], born_columns[tile, 0, rows, :], *partner
             )
         return carry
 
     lax.fori_loop(0, tiles, energy_near, 0)
     wait_all(born_window, born_send, born_recv)
+    over_window[...] = 1.0 / born_window[...]
+    charge_window[...] = window[3] * lax.rsqrt(born_window[...])
 
     def energy_far(tile, carry):
         for entry in range(1, width):
-            index, used = gather_partner(tile, entry)
-            row = jnp.where(used, row_of(born_window, index), 1.0)
-            partners[entry, 4] = row
-            partners[entry, 5] = 1.0 / row
+            index = lists[entry, tile]
+            partners[entry, 0] = row_of(over_window, index)
+            partners[entry, 1] = jnp.where(
+                entry < counts[tile], row_of(charge_window, index), 0.0
+            )
 
         def one_step(step, inner):
             rows = pl.ds(pl.multiple_of(step * ROWS, ROWS), ROWS)
-            own = [columns[tile, c, rows, :] for c in range(3)]
-            own_born = [born_columns[tile, c, rows, :] for c in range(2)]
+            own_column = born_columns[tile, 0, rows, :]
             total = sums[tile, 0, rows, :]
             for entry in range(1, width):
-                partner = [partners[entry, c] for c in range(6)]
                 total = total + energy_part(
-                    squared_distance(own, partner), *own_born, partner[4], partner[5], partner[3]
+                    distances[tile, entry, rows, :], own_column, partners[entry, 0], partners[entry, 1]
                 )
-            sums[tile, 0, rows, :] = total
+            collect(tile, rows, total)
             return inner
 
         lax.fori_loop(0, steps, one_step, 0, unroll=2)
-        result[pl.ds(tile, 1), :] = jnp.sum(sums[tile, 0].T, axis=0, keepdims=True)
         return carry
 
     lax.fori_loop(0, tiles, energy_far, 0)
 
-    energy = -0.5 * window[3, home, :] * result[...]
+    energy = -0.5 * charge_window[home, :] * collected_rows()
     energy_out[...] = energy
     total_window[pl.ds(me, 1), :] = jnp.sum(energy, axis=0, keepdims=True)
 
@@ -303,21 +334,33 @@
         width = tile_lists.shape[1]
         block = jax.ShapeDtypeStruct((tiles, LANES), jnp.float32)
         smem = pl.BlockSpec(memory_space=pltpu.SMEM)
+        hbm = pl.BlockSpec(memory_space=pltpu.HBM)
         vmem = pl.BlockSpec(memory_space=pltpu.VMEM)
         born, energy, total = pl.pallas_call(
             functools.partial(kernel, count),
             out_shape=(block, block, jax.ShapeDtypeStruct((1, 1), jnp.float32)),
-            in_specs=[smem] * 3 + [vmem] * 4,
+            in_specs=[hbm] * 7,
             out_specs=(vmem, vmem, smem),
             scratch_shapes=[
+                pltpu.SMEM((width, tiles), jnp.int32),
+                pltpu.SMEM((tiles,), jnp.int32),
+                pltpu.SMEM((1,), jnp.int32),
+                pltpu.VMEM(coords.shape, jnp.float32),
+                pltpu.VMEM((tiles, LANES), jnp.float32),
+                pltpu.VMEM((tiles, LANES), jnp.float32),
+                pltpu.VMEM((tiles, LANES), jnp.float32),
                 pltpu.VMEM((5, 5 * tiles, LANES), jnp.float32),
+                pltpu.VMEM((5 * tiles, LANES), jnp.float32),
+                pltpu.VMEM((5 * tiles, LANES), jnp.float32),
                 pltpu.VMEM((5 * tiles, LANES), jnp.float32),
                 pltpu.VMEM((count, LANES), jnp.float32),
                 pltpu.VMEM((tiles, 4, LANES, LANES), jnp.float32),
-                pltpu.VMEM((tiles, 2, LANES, LANES), jnp.float32),
-                pltpu.VMEM((width, 6, ROWS, LANES), jnp.float32),
+                pltpu.VMEM((tiles, 1, LANES, LANES), jnp.float32),
+                pltpu.VMEM((width, 4, ROWS, LANES), jnp.float32),
                 pltpu.VMEM((tiles, 3, LANES, LANES), jnp.float32),
-                pltpu.VMEM((tiles, LANES), jnp.float32),
+                pltpu.VMEM((tiles, width, LANES, LANES), jnp.float32),
+                pltpu.VMEM((LANES, LANES), jnp.float32),
+                pltpu.SemaphoreType.DMA((7,)),
                 pltpu.SemaphoreType.DMA((len(SHIFTS),)),
                 pltpu.SemaphoreType.DMA((len(SHIFTS),)),
                 pltpu.SemaphoreType.DMA((len(SHIFTS),)),
@@ -326,10 +369,11 @@
                 pltpu.SemaphoreType.DMA((count,)),
             ],
             compiler_params=pltpu.CompilerParams(
-                collective_id=0, has_side_effects=True, vmem_limit_bytes=40 * 1024 * 1024
+                collective_id=0, has_side_effects=True, vmem_limit_bytes=63463424
+
             ),
         )(
-            tile_lists,
+            tile_lists.T,
             tile_counts,
             slab_fill,
             coords,

time: 49.1 us -> 61 us (1.24)
  Pallas kernels: 42.4 us -> 55.6 us
  local copies, waits for them, and re-layouts: 3.44 us -> 1.99 us
    pallas_call x1, Pallas kernels: 42.4 us -> 55.6 us  [shards(): pl.pallas_call(functools.partial(kernel, count), out_shape=(block, block,...]
    unnamed x13 -> x6, local copies, waits for them, and re-layouts: 3.44 us -> 1.99 us
where the time goes in v2:
time: 61 us; the launch traced here: 60.7 us
  Pallas kernels  55.6 us (91%)
  between operations  3.04 us (5%)
  local copies, waits for them, and re-layouts  1.99 us (3%)
    pallas_call x1, Pallas kernels, shards(): pl.pallas_call(functools.partial(kernel, count), out_shape=(block, block,...  55.6 us
    unnamed x6, local copies, waits for them, and re-layouts  1.99 us

profile of v2, /device:TPU:0, one launch (start us, length us, event | category | flops | bytes accessed | tf_op | source)
XLA Modules:
  0.0 60.7 jit_solution(18249881182761058089)
XLA Ops:
  1.3 55.6 %shard_map.94 = (f32[16,128]{1,0:T(8,128)}, f32[16,128]{1,0:T(8,128)}, f32[1,1]{1,0:T(1,128)}) custom-call(s32[8,16]{1,0:T(8,128)} %bitcast.12, s32[16]{0:T(128)} %counts_in.1, s32[1]{0:T(128)S(6)} %copy.13.fill_in, f32[3,2048]{1,0:T(4,128)} %coords_in.1, f32[16,128]{1,0:T(8,128)} %bitcast.7, f32[16,128]{1,0:T(8,128)} %bitcast.8, f32[16,128]{1,0:T(8,128)} %bitcast.9), custom_call_target="tpu_custom_call" | custom-call | tf_op jit(solution)/shard_map/pallas_call | solution.py:339
  56.9 0.0 copy-start.1
  56.9 0.7 %copy-done.1 = f32[16,128]{1,0:T(8,128)S(1)} copy-done((f32[16,128]{1,0:T(8,128)S(1)}, f32[16,128]{1,0:T(8,128)}, u32[]{:S(2)}) %copy-start.1) | copy-done | bytes 8216
  57.6 0.0 copy-start
  57.6 0.6 copy.14
  58.2 0.1 copy-done
  58.3 0.6 copy.15
Async XLA Ops:
  56.9 0.7 %copy-start.1 = (f32[16,128]{1,0:T(8,128)S(1)}, f32[16,128]{1,0:T(8,128)}, u32[]{:S(2)}) copy-start(f32[16,128]{1,0:T(8,128)} %get-tuple-element.6) | copy-start | bytes 24580
  57.6 0.7 %copy-start = (f32[16,128]{1,0:T(8,128)S(1)}, f32[16,128]{1,0:T(8,128)}, u32[]{:S(2)}) copy-start(f32[16,128]{1,0:T(8,128)} %get-tuple-element.7) | copy-start | bytes 24580

commit v3 on v2

--- a/solution.py
+++ b/solution.py
@@ -80,7 +80,7 @@
     partners,
     sums,
     distances,
-    collected,
+    result,
     load_sems,
     window_send,
     window_recv,
@@ -190,15 +190,20 @@
     for component in range(3):
         spread_columns(window[component, home, :], columns, component)
     spread_columns(offset_own, columns, 3)
-    collected[...] = jnp.zeros((LANES, LANES), jnp.float32)
-
-    def collect(tile, rows, values):
-        lane = lax.broadcasted_iota(jnp.int32, (ROWS, LANES), 1)
-        row_sums = jnp.sum(values, axis=1, keepdims=True)
-        collected[rows, :] = jnp.where(lane == tile, row_sums, collected[rows, :])
-
-    def collected_rows():
-        return collected[...].T[:tiles, :]
+
+    ones = jnp.ones((ROWS, LANES), jnp.float32)
+
+    def row_sums():
+        for tile in range(tiles):
+            added = lax.dot_general(
+                ones,
+                sums[tile, 0],
+                (((1,), (1,)), ((), ())),
+                precision=lax.Precision.HIGHEST,
+                preferred_element_type=jnp.float32,
+            )
+            result[tile : tile + 1, :] = added[:1]
+        return result[...]
 
     def born_near(tile, carry):
         partner = [row_of(window.at[c], 2 * tiles + tile) for c in (0, 1, 2, 4)]
@@ -232,18 +237,18 @@
                 distances[tile, entry, rows, :] = squared
                 terms = born_parts(squared, own[3], partner[3])
                 totals = [old + term for old, term in zip(totals, terms)]
-            collect(
-                tile, rows, 0.125 * totals[0] + 0.25 * totals[1] + (2.0 / own[3]) * totals[2]
+            sums[tile, 0, rows, :] = (
+                0.125 * totals[0] + 0.25 * totals[1] + (2.0 / own[3]) * totals[2]
             )
             return inner
 
-        lax.fori_loop(0, steps, one_step, 0, unroll=2)
+        lax.fori_loop(0, steps, one_step, 0, unroll=4)
         return carry
 
     lax.fori_loop(0, tiles, born_far, 0)
 
     radius_own = jnp.where(live, radii[...], 1.5)
-    psi = collected_rows() * offset_own
+    psi = row_sums() * offset_own
     bending = jnp.tanh(psi - 0.8 * psi * psi + 4.85 * psi * psi * psi)
     born = 1.0 / (1.0 / offset_own - bending / radius_own)
     born_out[...] = jnp.where(live, born, 0.0)
@@ -285,15 +290,15 @@
                 total = total + energy_part(
                     distances[tile, entry, rows, :], own_column, partners[entry, 0], partners[entry, 1]
                 )
-            collect(tile, rows, total)
+            sums[tile, 0, rows, :] = total
             return inner
 
-        lax.fori_loop(0, steps, one_step, 0, unroll=2)
+        lax.fori_loop(0, steps, one_step, 0, unroll=4)
         return carry
 
     lax.fori_loop(0, tiles, energy_far, 0)
 
-    energy = -0.5 * charge_window[home, :] * collected_rows()
+    energy = -0.5 * charge_window[home, :] * row_sums()
     energy_out[...] = energy
     total_window[pl.ds(me, 1), :] = jnp.sum(energy, axis=0, keepdims=True)
 
@@ -324,6 +329,11 @@
     lax.fori_loop(1, count, total_wait, 0)
     total_out[0, 0] = jnp.sum(total_window[...])
     lax.fori_loop(1, count, total_sent, 0)
+
+
+def hand_over(born, energy, born_out, energy_out):
+    born_out[...] = born[...]
+    energy_out[...] = energy[...]
 
 
 def solution(mesh):
@@ -359,7 +369,7 @@
                 pltpu.VMEM((width, 4, ROWS, LANES), jnp.float32),
                 pltpu.VMEM((tiles, 3, LANES, LANES), jnp.float32),
                 pltpu.VMEM((tiles, width, LANES, LANES), jnp.float32),
-                pltpu.VMEM((LANES, LANES), jnp.float32),
+                pltpu.VMEM((tiles, LANES), jnp.float32),
                 pltpu.SemaphoreType.DMA((7,)),
                 pltpu.SemaphoreType.DMA((len(SHIFTS),)),
                 pltpu.SemaphoreType.DMA((len(SHIFTS),)),
@@ -381,6 +391,9 @@
             radii.reshape(tiles, LANES),
             screens.reshape(tiles, LANES),
         )
+        born, energy = pl.pallas_call(
+            hand_over, out_shape=(block, block), in_specs=[vmem] * 2, out_specs=(vmem, vmem)
+        )(born, energy)
         return born.reshape(-1), energy.reshape(-1), total.reshape(())
 
     placed = (

time: 61 us -> 42.2 us (0.69)
  Pallas kernels: 55.6 us -> 38.8 us
  local copies, waits for them, and re-layouts: 1.99 us -> 0 us
    pallas_call x1, Pallas kernels: 55.6 us -> 37.5 us  [shards(): pl.pallas_call(functools.partial(kernel, count), out_shape=(block, block,...]
    unnamed x6 -> x0, local copies, waits for them, and re-layouts: 1.99 us -> none
    pallas_call x0 -> x1, Pallas kernels: none -> 1.32 us  [shards(): pl.pallas_call(hand_over, out_shape=(block, block), in_specs=[vmem] * 2,...]
where the time goes in v3:
time: 42.2 us; the launch traced here: 41.9 us
  Pallas kernels  38.8 us (92%)
  between operations  3.02 us (7%)
    pallas_call x1, Pallas kernels, shards(): pl.pallas_call(functools.partial(kernel, count), out_shape=(block, block,...  37.5 us
    pallas_call x1, Pallas kernels, shards(): pl.pallas_call(hand_over, out_shape=(block, block), in_specs=[vmem] * 2,...  1.32 us

profile of v3, /device:TPU:0, one launch (start us, length us, event | category | flops | bytes accessed | tf_op | source)
XLA Modules:
  0.0 41.9 jit_solution(7006781981531491059)
XLA Ops:
  1.3 37.5 %shard_map.94 = (f32[16,128]{1,0:T(8,128)}, f32[16,128]{1,0:T(8,128)}, f32[1,1]{1,0:T(1,128)}) custom-call(s32[8,16]{1,0:T(8,128)} %bitcast.10, s32[16]{0:T(128)} %counts_in.1, s32[1]{0:T(128)S(6)} %copy.11.fill_in, f32[3,2048]{1,0:T(4,128)} %coords_in.1, f32[16,128]{1,0:T(8,128)} %bitcast.7, f32[16,128]{1,0:T(8,128)} %bitcast.8, f32[16,128]{1,0:T(8,128)} %bitcast.9), custom_call_target="tpu_custom_call" | custom-call | tf_op jit(solution)/shard_map/pallas_call | solution.py:349
  38.8 1.3 %shard_map.95 = (f32[16,128]{1,0:T(8,128)}, f32[16,128]{1,0:T(8,128)}) custom-call(f32[16,128]{1,0:T(8,128)} %get-tuple-element.8.born, f32[16,128]{1,0:T(8,128)} %get-tuple-element.9.energy), custom_call_target="tpu_custom_call" | custom-call | tf_op jit(solution)/shard_map/pallas_call | solution.py:394

commit v4 on v3

--- a/solution.py
+++ b/solution.py
@@ -80,7 +80,6 @@
     partners,
     sums,
     distances,
-    result,
     load_sems,
     window_send,
     window_recv,
@@ -191,19 +190,14 @@
         spread_columns(window[component, home, :], columns, component)
     spread_columns(offset_own, columns, 3)
 
-    ones = jnp.ones((ROWS, LANES), jnp.float32)
+    lane = lax.broadcasted_iota(jnp.int32, (LANES, LANES), 1)
 
     def row_sums():
+        gathered = jnp.zeros((LANES, LANES), jnp.float32)
         for tile in range(tiles):
-            added = lax.dot_general(
-                ones,
-                sums[tile, 0],
-                (((1,), (1,)), ((), ())),
-                precision=lax.Precision.HIGHEST,
-                preferred_element_type=jnp.float32,
-            )
-            result[tile : tile + 1, :] = added[:1]
-        return result[...]
+            added = jnp.sum(sums[tile, 0], axis=1, keepdims=True)
+            gathered = jnp.where(lane == tile, added, gathered)
+        return gathered.T[:tiles, :]
 
     def born_near(tile, carry):
         partner = [row_of(window.at[c], 2 * tiles + tile) for c in (0, 1, 2, 4)]
@@ -242,7 +236,7 @@
             )
             return inner
 
-        lax.fori_loop(0, steps, one_step, 0, unroll=4)
+        lax.fori_loop(0, steps, one_step, 0, unroll=steps)
         return carry
 
     lax.fori_loop(0, tiles, born_far, 0)
@@ -293,7 +287,7 @@
             sums[tile, 0, rows, :] = total
             return inner
 
-        lax.fori_loop(0, steps, one_step, 0, unroll=4)
+        lax.fori_loop(0, steps, one_step, 0, unroll=steps)
         return carry
 
     lax.fori_loop(0, tiles, energy_far, 0)
@@ -369,7 +363,6 @@
                 pltpu.VMEM((width, 4, ROWS, LANES), jnp.float32),
                 pltpu.VMEM((tiles, 3, LANES, LANES), jnp.float32),
                 pltpu.VMEM((tiles, width, LANES, LANES), jnp.float32),
-                pltpu.VMEM((tiles, LANES), jnp.float32),
                 pltpu.SemaphoreType.DMA((7,)),
                 pltpu.SemaphoreType.DMA((len(SHIFTS),)),
                 pltpu.SemaphoreType.DMA((len(SHIFTS),)),

time: 42.2 us -> 37.3 us (0.88)
  Pallas kernels: 38.8 us -> 33.9 us
    pallas_call x1, Pallas kernels: 37.5 us -> 32.6 us  [shards(): pl.pallas_call(functools.partial(kernel, count), out_shape=(block, block,...]
where the time goes in v4:
time: 37.3 us; the launch traced here: 36.9 us
  Pallas kernels  33.9 us (91%)
  between operations  3.02 us (8%)
    pallas_call x1, Pallas kernels, shards(): pl.pallas_call(functools.partial(kernel, count), out_shape=(block, block,...  32.6 us
    pallas_call x1, Pallas kernels, shards(): pl.pallas_call(hand_over, out_shape=(block, block), in_specs=[vmem] * 2,...  1.32 us

profile of v4, /device:TPU:0, one launch (start us, length us, event | category | flops | bytes accessed | tf_op | source)
XLA Modules:
  0.0 36.9 jit_solution(18330805146850149008)
XLA Ops:
  1.3 32.6 %shard_map.94 = (f32[16,128]{1,0:T(8,128)}, f32[16,128]{1,0:T(8,128)}, f32[1,1]{1,0:T(1,128)}) custom-call(s32[8,16]{1,0:T(8,128)} %bitcast.10, s32[16]{0:T(128)} %counts_in.1, s32[1]{0:T(128)S(6)} %copy.11.fill_in, f32[3,2048]{1,0:T(4,128)} %coords_in.1, f32[16,128]{1,0:T(8,128)} %bitcast.7, f32[16,128]{1,0:T(8,128)} %bitcast.8, f32[16,128]{1,0:T(8,128)} %bitcast.9), custom_call_target="tpu_custom_call" | custom-call | tf_op jit(solution)/shard_map/pallas_call | solution.py:343
  33.9 1.3 %shard_map.95 = (f32[16,128]{1,0:T(8,128)}, f32[16,128]{1,0:T(8,128)}) custom-call(f32[16,128]{1,0:T(8,128)} %get-tuple-element.8.born, f32[16,128]{1,0:T(8,128)} %get-tuple-element.9.energy), custom_call_target="tpu_custom_call" | custom-call | tf_op jit(solution)/shard_map/pallas_call | solution.py:387

commit v5 on v4

--- a/solution.py
+++ b/solution.py
@@ -23,7 +23,7 @@
     return dx * dx + dy * dy + dz * dz
 
 
-def born_parts(squared, offset_own, scaled, diagonal=None):
+def born_parts(squared, offset_own, scaled, scaled_square, diagonal=None):
     soft = squared + SOFTEN
     inverse = lax.rsqrt(soft)
     distance = soft * inverse
@@ -35,7 +35,7 @@
     over_lower = upper * both
     over_upper = lower * both
     apart = over_lower - over_upper
-    bend = distance - scaled * scaled * inverse
+    bend = distance - scaled_square * inverse
     first = apart * (4.0 - bend * (over_lower + over_upper))
     second = inverse * jnp.log(lower * over_upper)
     third = (inner - offset_own) * over_lower
@@ -201,35 +201,44 @@
 
     def born_near(tile, carry):
         partner = [row_of(window.at[c], 2 * tiles + tile) for c in (0, 1, 2, 4)]
+        scaled_square = partner[3] * partner[3]
         for step in range(steps):
             rows = pl.ds(step * ROWS, ROWS)
             own = [columns[tile, c, rows, :] for c in range(4)]
             squared = squared_distance(own, partner)
             distances[tile, 0, rows, :] = squared
-            terms = born_parts(squared, own[3], partner[3], diagonal_of(step * ROWS))
+            terms = born_parts(
+                squared, own[3], partner[3], scaled_square, diagonal_of(step * ROWS)
+            )
             for place, term in enumerate(terms):
                 sums[tile, place, rows, :] = term
         return carry
 
-    lax.fori_loop(0, tiles, born_near, 0)
+    lax.fori_loop(0, tiles, born_near, 0, unroll=2)
     wait_all(window, window_send, window_recv)
 
-    def born_far(tile, carry):
+    def born_gather(tile, carry):
         for entry in range(1, width):
             index = lists[entry, tile]
             for place in range(3):
-                partners[entry, place] = row_of(window.at[place], index)
-            partners[entry, 3] = jnp.where(entry < counts[tile], row_of(window.at[4], index), 0.0)
-
+                partners[tile, entry, place] = row_of(window.at[place], index)
+            scaled = jnp.where(entry < counts[tile], row_of(window.at[4], index), 0.0)
+            partners[tile, entry, 3] = scaled
+            partners[tile, entry, 4] = scaled * scaled
+        return carry
+
+    lax.fori_loop(0, tiles, born_gather, 0, unroll=4)
+
+    def born_far(tile, carry):
         def one_step(step, inner):
             rows = pl.ds(pl.multiple_of(step * ROWS, ROWS), ROWS)
             own = [columns[tile, c, rows, :] for c in range(4)]
             totals = [sums[tile, c, rows, :] for c in range(3)]
             for entry in range(1, width):
-                partner = [partners[entry, c] for c in range(4)]
+                partner = [partners[tile, entry, c] for c in range(5)]
                 squared = squared_distance(own, partner)
                 distances[tile, entry, rows, :] = squared
-                terms = born_parts(squared, own[3], partner[3])
+                terms = born_parts(squared, own[3], partner[3], partner[4])
                 totals = [old + term for old, term in zip(totals, terms)]
             sums[tile, 0, rows, :] = (
                 0.125 * totals[0] + 0.25 * totals[1] + (2.0 / own[3]) * totals[2]
@@ -263,26 +272,33 @@
             )
         return carry
 
-    lax.fori_loop(0, tiles, energy_near, 0)
+    lax.fori_loop(0, tiles, energy_near, 0, unroll=4)
     wait_all(born_window, born_send, born_recv)
     over_window[...] = 1.0 / born_window[...]
     charge_window[...] = window[3] * lax.rsqrt(born_window[...])
 
-    def energy_far(tile, carry):
+    def energy_gather(tile, carry):
         for entry in range(1, width):
             index = lists[entry, tile]
-            partners[entry, 0] = row_of(over_window, index)
-            partners[entry, 1] = jnp.where(
+            partners[tile, entry, 0] = row_of(over_window, index)
+            partners[tile, entry, 1] = jnp.where(
                 entry < counts[tile], row_of(charge_window, index), 0.0
             )
-
+        return carry
+
+    lax.fori_loop(0, tiles, energy_gather, 0, unroll=4)
+
+    def energy_far(tile, carry):
         def one_step(step, inner):
             rows = pl.ds(pl.multiple_of(step * ROWS, ROWS), ROWS)
             own_column = born_columns[tile, 0, rows, :]
             total = sums[tile, 0, rows, :]
             for entry in range(1, width):
                 total = total + energy_part(
-                    distances[tile, entry, rows, :], own_column, partners[entry, 0], partners[entry, 1]
+                    distances[tile, entry, rows, :],
+                    own_column,
+                    partners[tile, entry, 0],
+                    partners[tile, entry, 1],
                 )
             sums[tile, 0, rows, :] = total
             return inner
@@ -325,9 +341,15 @@
     lax.fori_loop(1, count, total_sent, 0)
 
 
-def hand_over(born, energy, born_out, energy_out):
-    born_out[...] = born[...]
-    energy_out[...] = energy[...]
+def hand_over(born, energy, born_out, energy_out, sems):
+    copies = [
+        pltpu.make_async_copy(born, born_out, sems.at[0]),
+        pltpu.make_async_copy(energy, energy_out, sems.at[1]),
+    ]
+    for copy in copies:
+        copy.start()
+    for copy in copies:
+        copy.wait()
 
 
 def solution(mesh):
@@ -360,7 +382,7 @@
                 pltpu.VMEM((count, LANES), jnp.float32),
                 pltpu.VMEM((tiles, 4, LANES, LANES), jnp.float32),
                 pltpu.VMEM((tiles, 1, LANES, LANES), jnp.float32),
-                pltpu.VMEM((width, 4, ROWS, LANES), jnp.float32),
+                pltpu.VMEM((tiles, width, 5, ROWS, LANES), jnp.float32),
                 pltpu.VMEM((tiles, 3, LANES, LANES), jnp.float32),
                 pltpu.VMEM((tiles, width, LANES, LANES), jnp.float32),
                 pltpu.SemaphoreType.DMA((7,)),
@@ -385,7 +407,11 @@
             screens.reshape(tiles, LANES),
         )
         born, energy = pl.pallas_call(
-            hand_over, out_shape=(block, block), in_specs=[vmem] * 2, out_specs=(vmem, vmem)
+            hand_over,
+            out_shape=(block, block),
+            in_specs=[hbm] * 2,
+            out_specs=(hbm, hbm),
+            scratch_shapes=[pltpu.SemaphoreType.DMA((2,))],
         )(born, energy)
         return born.reshape(-1), energy.reshape(-1), total.reshape(())
 

time: 37.3 us -> 37.5 us (level)
  no operation moved by 1% of the time
where the time goes in v5:
time: 37.5 us; the launch traced here: 37.3 us
  Pallas kernels  34.2 us (91%)
  between operations  3.03 us (8%)
    pallas_call x1, Pallas kernels, shards(): pl.pallas_call(functools.partial(kernel, count), out_shape=(block, block,...  32.6 us
    pallas_call x1, Pallas kernels, shards(): pl.pallas_call(hand_over, out_shape=(block, block), in_specs=[hbm] * 2, o...  1.62 us

profile of v5, /device:TPU:0, one launch (start us, length us, event | category | flops | bytes accessed | tf_op | source)
XLA Modules:
  0.0 37.3 jit_solution(224761647478137459)
XLA Ops:
  1.3 32.6 %shard_map.94 = (f32[16,128]{1,0:T(8,128)}, f32[16,128]{1,0:T(8,128)}, f32[1,1]{1,0:T(1,128)}) custom-call(s32[8,16]{1,0:T(8,128)} %bitcast.10, s32[16]{0:T(128)} %counts_in.1, s32[1]{0:T(128)S(6)} %copy.11.fill_in, f32[3,2048]{1,0:T(4,128)} %coords_in.1, f32[16,128]{1,0:T(8,128)} %bitcast.7, f32[16,128]{1,0:T(8,128)} %bitcast.8, f32[16,128]{1,0:T(8,128)} %bitcast.9), custom_call_target="tpu_custom_call" | custom-call | tf_op jit(solution)/shard_map/pallas_call | solution.py:365
  33.9 1.6 %shard_map.95 = (f32[16,128]{1,0:T(8,128)}, f32[16,128]{1,0:T(8,128)}) custom-call(f32[16,128]{1,0:T(8,128)} %get-tuple-element.8.born, f32[16,128]{1,0:T(8,128)} %get-tuple-element.9.energy), custom_call_target="tpu_custom_call" | custom-call | tf_op jit(solution)/shard_map/pallas_call | solution.py:409

commit v6 on v5

--- a/solution.py
+++ b/solution.py
@@ -16,15 +16,12 @@
 ROWS = 8
 
 
-def squared_distance(own, partner):
-    dx = own[0] - partner[0]
-    dy = own[1] - partner[1]
-    dz = own[2] - partner[2]
-    return dx * dx + dy * dy + dz * dz
-
-
-def born_parts(squared, offset_own, scaled, scaled_square, diagonal=None):
-    soft = squared + SOFTEN
+def softened_distance(own, partner):
+    total = (own[3] + partner[3]) + own[0] * partner[0]
+    return (total + own[1] * partner[1]) + own[2] * partner[2]
+
+
+def born_parts(soft, offset_own, scaled, scaled_square, diagonal=None):
     inverse = lax.rsqrt(soft)
     distance = soft * inverse
     upper = distance + scaled
@@ -46,8 +43,8 @@
     return first, second, third
 
 
-def energy_part(squared, own_over, partner_over, partner_charge):
-    scaled = squared * (own_over * partner_over)
+def energy_part(soft, own_over, partner_over, partner_charge):
+    scaled = (soft - SOFTEN) * (own_over * partner_over)
     return partner_charge * lax.rsqrt(scaled + jnp.exp2(scaled * (-0.25 * LOG2E)))
 
 
@@ -71,6 +68,7 @@
     radii,
     screens,
     window,
+    places,
     born_window,
     over_window,
     charge_window,
@@ -186,9 +184,22 @@
         for tile in range(tiles):
             block[tile, place] = jnp.broadcast_to(turned[:, tile : tile + 1], (LANES, LANES))
 
+    middle = 2 * tiles + tiles // 2
+    centre = [window[c, middle : middle + 1, :1] for c in range(3)]
+
+    def place_around(rows):
+        length = jnp.zeros((rows.size, LANES), jnp.float32)
+        for component in range(3):
+            moved = window[component, rows, :] - centre[component]
+            places[component, rows, :] = moved
+            length = length + moved * moved
+        places[3, rows, :] = length
+
+    place_around(home)
     for component in range(3):
-        spread_columns(window[component, home, :], columns, component)
-    spread_columns(offset_own, columns, 3)
+        spread_columns(-2.0 * places[component, home, :], columns, component)
+    spread_columns(places[3, home, :] + SOFTEN, columns, 3)
+    spread_columns(offset_own, columns, 4)
 
     lane = lax.broadcasted_iota(jnp.int32, (LANES, LANES), 1)
 
@@ -200,31 +211,33 @@
         return gathered.T[:tiles, :]
 
     def born_near(tile, carry):
-        partner = [row_of(window.at[c], 2 * tiles + tile) for c in (0, 1, 2, 4)]
-        scaled_square = partner[3] * partner[3]
+        partner = [row_of(places.at[c], 2 * tiles + tile) for c in range(4)]
+        scaled = row_of(window.at[4], 2 * tiles + tile)
+        scaled_square = scaled * scaled
         for step in range(steps):
             rows = pl.ds(step * ROWS, ROWS)
-            own = [columns[tile, c, rows, :] for c in range(4)]
-            squared = squared_distance(own, partner)
-            distances[tile, 0, rows, :] = squared
-            terms = born_parts(
-                squared, own[3], partner[3], scaled_square, diagonal_of(step * ROWS)
-            )
+            own = [columns[tile, c, rows, :] for c in range(5)]
+            diagonal = diagonal_of(step * ROWS)
+            soft = jnp.where(diagonal, SOFTEN, softened_distance(own, partner))
+            distances[tile, 0, rows, :] = soft
+            terms = born_parts(soft, own[4], scaled, scaled_square, diagonal)
             for place, term in enumerate(terms):
                 sums[tile, place, rows, :] = term
         return carry
 
-    lax.fori_loop(0, tiles, born_near, 0, unroll=2)
+    lax.fori_loop(0, tiles, born_near, 0)
     wait_all(window, window_send, window_recv)
+    place_around(pl.ds(0, 2 * tiles))
+    place_around(pl.ds(3 * tiles, 2 * tiles))
 
     def born_gather(tile, carry):
         for entry in range(1, width):
             index = lists[entry, tile]
-            for place in range(3):
-                partners[tile, entry, place] = row_of(window.at[place], index)
+            for place in range(4):
+                partners[tile, entry, place] = row_of(places.at[place], index)
             scaled = jnp.where(entry < counts[tile], row_of(window.at[4], index), 0.0)
-            partners[tile, entry, 3] = scaled
-            partners[tile, entry, 4] = scaled * scaled
+            partners[tile, entry, 4] = scaled
+            partners[tile, entry, 5] = scaled * scaled
         return carry
 
     lax.fori_loop(0, tiles, born_gather, 0, unroll=4)
@@ -232,20 +245,20 @@
     def born_far(tile, carry):
         def one_step(step, inner):
             rows = pl.ds(pl.multiple_of(step * ROWS, ROWS), ROWS)
-            own = [columns[tile, c, rows, :] for c in range(4)]
+            own = [columns[tile, c, rows, :] for c in range(5)]
             totals = [sums[tile, c, rows, :] for c in range(3)]
             for entry in range(1, width):
-                partner = [partners[tile, entry, c] for c in range(5)]
-                squared = squared_distance(own, partner)
-                distances[tile, entry, rows, :] = squared
-                terms = born_parts(squared, own[3], partner[3], partner[4])
+                partner = [partners[tile, entry, c] for c in range(6)]
+                soft = softened_distance(own, partner)
+                distances[tile, entry, rows, :] = soft
+                terms = born_parts(soft, own[4], partner[4], partner[5])
                 totals = [old + term for old, term in zip(totals, terms)]
             sums[tile, 0, rows, :] = (
-                0.125 * totals[0] + 0.25 * totals[1] + (2.0 / own[3]) * totals[2]
+                0.125 * totals[0] + 0.25 * totals[1] + (2.0 / own[4]) * totals[2]
             )
             return inner
 
-        lax.fori_loop(0, steps, one_step, 0, unroll=steps)
+        lax.fori_loop(0, steps, one_step, 0, unroll=8)
         return carry
 
     lax.fori_loop(0, tiles, born_far, 0)
@@ -272,7 +285,7 @@
             )
         return carry
 
-    lax.fori_loop(0, tiles, energy_near, 0, unroll=4)
+    lax.fori_loop(0, tiles, energy_near, 0)
     wait_all(born_window, born_send, born_recv)
     over_window[...] = 1.0 / born_window[...]
     charge_window[...] = window[3] * lax.rsqrt(born_window[...])
@@ -303,7 +316,7 @@
             sums[tile, 0, rows, :] = total
             return inner
 
-        lax.fori_loop(0, steps, one_step, 0, unroll=steps)
+        lax.fori_loop(0, steps, one_step, 0, unroll=8)
         return carry
 
     lax.fori_loop(0, tiles, energy_far, 0)
@@ -341,15 +354,9 @@
     lax.fori_loop(1, count, total_sent, 0)
 
 
-def hand_over(born, energy, born_out, energy_out, sems):
-    copies = [
-        pltpu.make_async_copy(born, born_out, sems.at[0]),
-        pltpu.make_async_copy(energy, energy_out, sems.at[1]),
-    ]
-    for copy in copies:
-        copy.start()
-    for copy in copies:
-        copy.wait()
+def hand_over(born, energy, born_out, energy_out):
+    born_out[...] = born[...]
+    energy_out[...] = energy[...]
 
 
 def solution(mesh):
@@ -376,13 +383,14 @@
                 pltpu.VMEM((tiles, LANES), jnp.float32),
                 pltpu.VMEM((tiles, LANES), jnp.float32),
                 pltpu.VMEM((5, 5 * tiles, LANES), jnp.float32),
+                pltpu.VMEM((4, 5 * tiles, LANES), jnp.float32),
                 pltpu.VMEM((5 * tiles, LANES), jnp.float32),
                 pltpu.VMEM((5 * tiles, LANES), jnp.float32),
                 pltpu.VMEM((5 * tiles, LANES), jnp.float32),
                 pltpu.VMEM((count, LANES), jnp.float32),
-                pltpu.VMEM((tiles, 4, LANES, LANES), jnp.float32),
+                pltpu.VMEM((tiles, 5, LANES, LANES), jnp.float32),
                 pltpu.VMEM((tiles, 1, LANES, LANES), jnp.float32),
-                pltpu.VMEM((tiles, width, 5, ROWS, LANES), jnp.float32),
+                pltpu.VMEM((tiles, width, 6, ROWS, LANES), jnp.float32),
                 pltpu.VMEM((tiles, 3, LANES, LANES), jnp.float32),
                 pltpu.VMEM((tiles, width, LANES, LANES), jnp.float32),
                 pltpu.SemaphoreType.DMA((7,)),
@@ -409,9 +417,8 @@
         born, energy = pl.pallas_call(
             hand_over,
             out_shape=(block, block),
-            in_specs=[hbm] * 2,
-            out_specs=(hbm, hbm),
-            scratch_shapes=[pltpu.SemaphoreType.DMA((2,))],
+            in_specs=[vmem] * 2,
+            out_specs=(vmem, vmem),
         )(born, energy)
         return born.reshape(-1), energy.reshape(-1), total.reshape(())
 

time: 37.5 us -> 38.1 us (1.016)
  Pallas kernels: 34.2 us -> 34.7 us
    pallas_call x1, Pallas kernels: 32.6 us -> 33.3 us  [shards(): pl.pallas_call(functools.partial(kernel, count), out_shape=(block, block,...]
where the time goes in v6:
time: 38.1 us; the launch traced here: 37.7 us
  Pallas kernels  34.7 us (91%)
  between operations  3.02 us (8%)
    pallas_call x1, Pallas kernels, shards(): pl.pallas_call(functools.partial(kernel, count), out_shape=(block, block,...  33.3 us
    pallas_call x1, Pallas kernels, shards(): pl.pallas_call(hand_over, out_shape=(block, block), in_specs=[vmem] * 2,...  1.32 us

profile of v6, /device:TPU:0, one launch (start us, length us, event | category | flops | bytes accessed | tf_op | source)
XLA Modules:
  0.0 37.7 jit_solution(293542315812824902)
XLA Ops:
  1.3 33.3 %shard_map.94 = (f32[16,128]{1,0:T(8,128)}, f32[16,128]{1,0:T(8,128)}, f32[1,1]{1,0:T(1,128)}) custom-call(s32[8,16]{1,0:T(8,128)} %bitcast.10, s32[16]{0:T(128)} %counts_in.1, s32[1]{0:T(128)S(6)} %copy.11.fill_in, f32[3,2048]{1,0:T(4,128)} %coords_in.1, f32[16,128]{1,0:T(8,128)} %bitcast.7, f32[16,128]{1,0:T(8,128)} %bitcast.8, f32[16,128]{1,0:T(8,128)} %bitcast.9), custom_call_target="tpu_custom_call" | custom-call | tf_op jit(solution)/shard_map/pallas_call | solution.py:372
  34.6 1.3 %shard_map.95 = (f32[16,128]{1,0:T(8,128)}, f32[16,128]{1,0:T(8,128)}) custom-call(f32[16,128]{1,0:T(8,128)} %get-tuple-element.8.born, f32[16,128]{1,0:T(8,128)} %get-tuple-element.9.energy), custom_call_target="tpu_custom_call" | custom-call | tf_op jit(solution)/shard_map/pallas_call | solution.py:417

commit v7 on v6

--- a/solution.py
+++ b/solution.py
@@ -21,26 +21,46 @@
     return (total + own[1] * partner[1]) + own[2] * partner[2]
 
 
-def born_parts(soft, offset_own, scaled, scaled_square, diagonal=None):
-    inverse = lax.rsqrt(soft)
-    distance = soft * inverse
-    upper = distance + scaled
-    reach = distance - scaled
-    inner = jnp.maximum(offset_own, scaled - distance)
-    lower = jnp.minimum(jnp.maximum(inner, reach), upper)
-    both = pl.reciprocal(upper * lower, approx=True)
-    over_lower = upper * both
-    over_upper = lower * both
-    apart = over_lower - over_upper
-    bend = distance - scaled_square * inverse
-    first = apart * (4.0 - bend * (over_lower + over_upper))
-    second = inverse * jnp.log(lower * over_upper)
-    third = (inner - offset_own) * over_lower
-    if diagonal is not None:
-        first = jnp.where(diagonal, 0.0, first)
-        second = jnp.where(diagonal, 0.0, second)
-        third = jnp.where(diagonal, 0.0, third)
-    return first, second, third
+def reciprocals(values):
+    if len(values) == 1:
+        return [pl.reciprocal(values[0], approx=True)]
+    if len(values) == 2:
+        both = pl.reciprocal(values[0] * values[1], approx=True)
+        return [both * values[1], both * values[0]]
+    if len(values) > 4:
+        return reciprocals(values[:4]) + reciprocals(values[4:])
+    pair = values[0] * values[1]
+    rest = values[2] * values[3] if len(values) == 4 else values[2]
+    whole = pl.reciprocal(pair * rest, approx=True)
+    over_pair, over_rest = whole * rest, whole * pair
+    first = [over_pair * values[1], over_pair * values[0]]
+    if len(values) == 3:
+        return first + [over_rest]
+    return first + [over_rest * values[3], over_rest * values[2]]
+
+
+def born_parts(softs, offsets, scaled, squares):
+    shapes = []
+    for soft, offset_own, radius in zip(softs, offsets, scaled):
+        inverse = lax.rsqrt(soft)
+        distance = soft * inverse
+        upper = distance + radius
+        inner = jnp.maximum(offset_own, radius - distance)
+        lower = jnp.minimum(jnp.maximum(inner, distance - radius), upper)
+        shapes.append((inverse, distance, upper, inner, lower))
+    both = reciprocals([upper * lower for _, _, upper, _, lower in shapes])
+    terms = []
+    for (inverse, distance, upper, inner, lower), over, offset_own, square in zip(
+        shapes, both, offsets, squares
+    ):
+        over_lower = upper * over
+        over_upper = lower * over
+        bend = distance - square * inverse
+        first = (over_lower - over_upper) * (4.0 - bend * (over_lower + over_upper))
+        second = inverse * jnp.log(lower * over_upper)
+        third = (inner - offset_own) * over_lower
+        terms.append((first, second, third))
+    return terms
 
 
 def energy_part(soft, own_over, partner_over, partner_charge):
@@ -214,15 +234,21 @@
         partner = [row_of(places.at[c], 2 * tiles + tile) for c in range(4)]
         scaled = row_of(window.at[4], 2 * tiles + tile)
         scaled_square = scaled * scaled
-        for step in range(steps):
-            rows = pl.ds(step * ROWS, ROWS)
-            own = [columns[tile, c, rows, :] for c in range(5)]
-            diagonal = diagonal_of(step * ROWS)
-            soft = jnp.where(diagonal, SOFTEN, softened_distance(own, partner))
-            distances[tile, 0, rows, :] = soft
-            terms = born_parts(soft, own[4], scaled, scaled_square, diagonal)
-            for place, term in enumerate(terms):
-                sums[tile, place, rows, :] = term
+        for start in range(0, steps, 4):
+            softs, offsets, marks = [], [], []
+            for step in range(start, start + 4):
+                rows = pl.ds(step * ROWS, ROWS)
+                own = [columns[tile, c, rows, :] for c in range(5)]
+                diagonal = diagonal_of(step * ROWS)
+                soft = jnp.where(diagonal, SOFTEN, softened_distance(own, partner))
+                distances[tile, 0, rows, :] = soft
+                softs.append(soft)
+                offsets.append(own[4])
+                marks.append(diagonal)
+            parts = born_parts(softs, offsets, [scaled] * 4, [scaled_square] * 4)
+            for step, diagonal, terms in zip(range(start, start + 4), marks, parts):
+                for place, term in enumerate(terms):
+                    sums[tile, place, pl.ds(step * ROWS, ROWS), :] = jnp.where(diagonal, 0.0, term)
         return carry
 
     lax.fori_loop(0, tiles, born_near, 0)
@@ -247,12 +273,18 @@
             rows = pl.ds(pl.multiple_of(step * ROWS, ROWS), ROWS)
             own = [columns[tile, c, rows, :] for c in range(5)]
             totals = [sums[tile, c, rows, :] for c in range(3)]
-            for entry in range(1, width):
-                partner = [partners[tile, entry, c] for c in range(6)]
-                soft = softened_distance(own, partner)
-                distances[tile, entry, rows, :] = soft
-                terms = born_parts(soft, own[4], partner[4], partner[5])
-                totals = [old + term for old, term in zip(totals, terms)]
+            for first in range(1, width, 4):
+                entries = range(first, min(first + 4, width))
+                softs, scaled, squares = [], [], []
+                for entry in entries:
+                    partner = [partners[tile, entry, c] for c in range(6)]
+                    soft = softened_distance(own, partner)
+                    distances[tile, entry, rows, :] = soft
+                    softs.append(soft)
+                    scaled.append(partner[4])
+                    squares.append(partner[5])
+                for terms in born_parts(softs, [own[4]] * len(softs), scaled, squares):
+                    totals = [old + term for old, term in zip(totals, terms)]
             sums[tile, 0, rows, :] = (
                 0.125 * totals[0] + 0.25 * totals[1] + (2.0 / own[4]) * totals[2]
             )

time: 38.1 us -> 38.5 us (1.010)
  Pallas kernels: 34.7 us -> 35.1 us
    pallas_call x1, Pallas kernels: 33.3 us -> 33.8 us  [shards(): pl.pallas_call(functools.partial(kernel, count), out_shape=(block, block,...]
where the time goes in v7:
time: 38.5 us; the launch traced here: 38.1 us
  Pallas kernels  35.1 us (91%)
  between operations  3.02 us (8%)
    pallas_call x1, Pallas kernels, shards(): pl.pallas_call(functools.partial(kernel, count), out_shape=(block, block,...  33.8 us
    pallas_call x1, Pallas kernels, shards(): pl.pallas_call(hand_over, out_shape=(block, block), in_specs=[vmem] * 2,...  1.32 us

profile of v7, /device:TPU:0, one launch (start us, length us, event | category | flops | bytes accessed | tf_op | source)
XLA Modules:
  0.0 38.1 jit_solution(11813475309031806764)
XLA Ops:
  1.3 33.8 %shard_map.94 = (f32[16,128]{1,0:T(8,128)}, f32[16,128]{1,0:T(8,128)}, f32[1,1]{1,0:T(1,128)}) custom-call(s32[8,16]{1,0:T(8,128)} %bitcast.10, s32[16]{0:T(128)} %counts_in.1, s32[1]{0:T(128)S(6)} %copy.11.fill_in, f32[3,2048]{1,0:T(4,128)} %coords_in.1, f32[16,128]{1,0:T(8,128)} %bitcast.7, f32[16,128]{1,0:T(8,128)} %bitcast.8, f32[16,128]{1,0:T(8,128)} %bitcast.9), custom_call_target="tpu_custom_call" | custom-call | tf_op jit(solution)/shard_map/pallas_call | solution.py:404
  35.0 1.3 %shard_map.95 = (f32[16,128]{1,0:T(8,128)}, f32[16,128]{1,0:T(8,128)}) custom-call(f32[16,128]{1,0:T(8,128)} %get-tuple-element.8.born, f32[16,128]{1,0:T(8,128)} %get-tuple-element.9.energy), custom_call_target="tpu_custom_call" | custom-call | tf_op jit(solution)/shard_map/pallas_call | solution.py:449

commit v8 on v6

--- a/solution.py
+++ b/solution.py
@@ -50,6 +50,7 @@
 
 def kernel(
     count,
+    group,
     lists_in,
     counts_in,
     fill_in,
@@ -72,7 +73,8 @@
     born_window,
     over_window,
     charge_window,
-    total_window,
+    near_window,
+    far_window,
     columns,
     born_columns,
     partners,
@@ -83,8 +85,10 @@
     window_recv,
     born_send,
     born_recv,
-    total_send,
-    total_recv,
+    near_send,
+    near_recv,
+    far_send,
+    far_recv,
 ):
     me = lax.axis_index("slab")
     tiles = charges.shape[0]
@@ -110,13 +114,20 @@
 
     barrier = pltpu.get_barrier_semaphore()
 
-    def greet(step, carry):
-        pl.semaphore_signal(
-            barrier, inc=1, device_id=(lax.rem(me + step, count),), device_id_type=MESH
-        )
-        return carry
-
-    lax.fori_loop(1, count, greet, 0)
+    def there(shift):
+        return jnp.logical_and(me + shift >= 0, me + shift < count)
+
+    def greet(device):
+        pl.semaphore_signal(barrier, inc=1, device_id=(device,), device_id_type=MESH)
+
+    rank = lax.rem(me, group)
+    first = me - rank
+    near_peers = [first + lax.rem(rank + step, group) for step in range(1, group)]
+    far_peers = [lax.rem(me + step * group, count) for step in range(1, count // group)]
+    for shift in SHIFTS:
+        pl.when(there(shift))(functools.partial(greet, me + shift))
+    for peer in near_peers + far_peers:
+        greet(peer)
     for load in loads:
         load.wait()
 
@@ -133,9 +144,6 @@
     window[3, home, :] = jnp.where(live, charges[...], 0.0)
     window[4, home, :] = jnp.where(live, screens[...] * (radii[...] - OFFSET), 0.0)
 
-    def there(shift):
-        return jnp.logical_and(me + shift >= 0, me + shift < count)
-
     def send(buffer, sems_out, sems_in, place, shift):
         def view(spot):
             rows = pl.ds(spot * tiles, tiles)
@@ -169,7 +177,10 @@
             window[:, rows, :] = jnp.zeros((5, tiles, LANES), jnp.float32)
             born_window[rows, :] = jnp.ones((tiles, LANES), jnp.float32)
 
-    pl.semaphore_wait(barrier, count - 1)
+    greetings = len(near_peers) + len(far_peers)
+    for shift in SHIFTS:
+        greetings = greetings + there(shift).astype(jnp.int32)
+    pl.semaphore_wait(barrier, greetings)
     send_all(window, window_send, window_recv)
 
     def diagonal_of(row):
@@ -258,7 +269,7 @@
             )
             return inner
 
-        lax.fori_loop(0, steps, one_step, 0, unroll=8)
+        lax.fori_loop(0, steps, one_step, 0, unroll=steps)
         return carry
 
     lax.fori_loop(0, tiles, born_far, 0)
@@ -316,42 +327,42 @@
             sums[tile, 0, rows, :] = total
             return inner
 
-        lax.fori_loop(0, steps, one_step, 0, unroll=8)
+        lax.fori_loop(0, steps, one_step, 0, unroll=steps)
         return carry
 
     lax.fori_loop(0, tiles, energy_far, 0)
 
     energy = -0.5 * charge_window[home, :] * row_sums()
     energy_out[...] = energy
-    total_window[pl.ds(me, 1), :] = jnp.sum(energy, axis=0, keepdims=True)
-
-    def total_copy(step):
-        mine = total_window.at[pl.ds(me, 1), :]
-        return pltpu.make_async_remote_copy(
-            src_ref=mine,
-            dst_ref=mine,
-            send_sem=total_send.at[step],
-            recv_sem=total_recv.at[step],
-            device_id=(lax.rem(me + step, count),),
-            device_id_type=MESH,
-        )
-
-    def total_start(step, carry):
-        total_copy(step).start()
-        return carry
-
-    def total_wait(step, carry):
-        total_copy(step).wait_recv()
-        return carry
-
-    def total_sent(step, carry):
-        total_copy(step).wait_send()
-        return carry
-
-    lax.fori_loop(1, count, total_start, 0)
-    lax.fori_loop(1, count, total_wait, 0)
-    total_out[0, 0] = jnp.sum(total_window[...])
-    lax.fori_loop(1, count, total_sent, 0)
+
+    def exchange(row, buffer, place, peers, sems_out, sems_in):
+        mine = buffer.at[pl.ds(place, 1), :]
+        buffer[pl.ds(place, 1), :] = row
+        copies = [
+            pltpu.make_async_remote_copy(
+                src_ref=mine,
+                dst_ref=mine,
+                send_sem=sems_out.at[index],
+                recv_sem=sems_in.at[index],
+                device_id=(peer,),
+                device_id_type=MESH,
+            )
+            for index, peer in enumerate(peers)
+        ]
+        for copy in copies:
+            copy.start()
+        for copy in copies:
+            copy.wait_recv()
+        return jnp.sum(buffer[...], axis=0, keepdims=True), copies
+
+    row = jnp.sum(energy, axis=0, keepdims=True)
+    row, near_copies = exchange(row, near_window, rank, near_peers, near_send, near_recv)
+    row, far_copies = exchange(
+        row, far_window, lax.div(me, group), far_peers, far_send, far_recv
+    )
+    total_out[0, 0] = jnp.sum(row)
+    for copy in near_copies + far_copies:
+        copy.wait_send()
 
 
 def hand_over(born, energy, born_out, energy_out):
@@ -361,6 +372,7 @@
 
 def solution(mesh):
     count = mesh.shape["slab"]
+    group = next(size for size in range(1, count + 1) if count % size == 0 and size * size >= count)
 
     def shards(coords, charges, radii, screens, tile_lists, tile_counts, slab_fill):
         tiles = charges.shape[0] // LANES
@@ -370,7 +382,7 @@
         hbm = pl.BlockSpec(memory_space=pltpu.HBM)
         vmem = pl.BlockSpec(memory_space=pltpu.VMEM)
         born, energy, total = pl.pallas_call(
-            functools.partial(kernel, count),
+            functools.partial(kernel, count, group),
             out_shape=(block, block, jax.ShapeDtypeStruct((1, 1), jnp.float32)),
             in_specs=[hbm] * 7,
             out_specs=(vmem, vmem, smem),
@@ -387,7 +399,8 @@
                 pltpu.VMEM((5 * tiles, LANES), jnp.float32),
                 pltpu.VMEM((5 * tiles, LANES), jnp.float32),
                 pltpu.VMEM((5 * tiles, LANES), jnp.float32),
-                pltpu.VMEM((count, LANES), jnp.float32),
+                pltpu.VMEM((group, LANES), jnp.float32),
+                pltpu.VMEM((count // group, LANES), jnp.float32),
                 pltpu.VMEM((tiles, 5, LANES, LANES), jnp.float32),
                 pltpu.VMEM((tiles, 1, LANES, LANES), jnp.float32),
                 pltpu.VMEM((tiles, width, 6, ROWS, LANES), jnp.float32),
@@ -398,8 +411,10 @@
                 pltpu.SemaphoreType.DMA((len(SHIFTS),)),
                 pltpu.SemaphoreType.DMA((len(SHIFTS),)),
                 pltpu.SemaphoreType.DMA((len(SHIFTS),)),
-                pltpu.SemaphoreType.DMA((count,)),
-                pltpu.SemaphoreType.DMA((count,)),
+                pltpu.SemaphoreType.DMA((group,)),
+                pltpu.SemaphoreType.DMA((group,)),
+                pltpu.SemaphoreType.DMA((count // group,)),
+                pltpu.SemaphoreType.DMA((count // group,)),
             ],
             compiler_params=pltpu.CompilerParams(
                 collective_id=0, has_side_effects=True, vmem_limit_bytes=63463424

time: 38.1 us -> 38.3 us (level)
  no operation moved by 1% of the time
where the time goes in v8:
time: 38.3 us; the launch traced here: 38 us
  Pallas kernels  34.9 us (91%)
  between operations  3.02 us (8%)
    pallas_call x1, Pallas kernels, shards(): pl.pallas_call(functools.partial(kernel, count, group), out_shape=(block,...  33.6 us
    pallas_call x1, Pallas kernels, shards(): pl.pallas_call(hand_over, out_shape=(block, block), in_specs=[vmem] * 2,...  1.32 us

profile of v8, /device:TPU:0, one launch (start us, length us, event | category | flops | bytes accessed | tf_op | source)
XLA Modules:
  0.0 38.0 jit_solution(11668126648616663300)
XLA Ops:
  1.3 33.6 %shard_map.94 = (f32[16,128]{1,0:T(8,128)}, f32[16,128]{1,0:T(8,128)}, f32[1,1]{1,0:T(1,128)}) custom-call(s32[8,16]{1,0:T(8,128)} %bitcast.10, s32[16]{0:T(128)} %counts_in.1, s32[1]{0:T(128)S(6)} %copy.11.fill_in, f32[3,2048]{1,0:T(4,128)} %coords_in.1, f32[16,128]{1,0:T(8,128)} %bitcast.7, f32[16,128]{1,0:T(8,128)} %bitcast.8, f32[16,128]{1,0:T(8,128)} %bitcast.9), custom_call_target="tpu_custom_call" | custom-call | tf_op jit(solution)/shard_map/pallas_call | solution.py:384
  34.9 1.3 %shard_map.95 = (f32[16,128]{1,0:T(8,128)}, f32[16,128]{1,0:T(8,128)}) custom-call(f32[16,128]{1,0:T(8,128)} %get-tuple-element.8.born, f32[16,128]{1,0:T(8,128)} %get-tuple-element.9.energy), custom_call_target="tpu_custom_call" | custom-call | tf_op jit(solution)/shard_map/pallas_call | solution.py:432

commit v9 on v4

--- a/solution.py
+++ b/solution.py
@@ -222,21 +222,23 @@
             partners[entry, 3] = jnp.where(entry < counts[tile], row_of(window.at[4], index), 0.0)
 
         def one_step(step, inner):
-            rows = pl.ds(pl.multiple_of(step * ROWS, ROWS), ROWS)
-            own = [columns[tile, c, rows, :] for c in range(4)]
-            totals = [sums[tile, c, rows, :] for c in range(3)]
+            spots = [pl.ds((step * 4 + part) * ROWS, ROWS) for part in range(4)]
+            owns = [[columns[tile, c, rows, :] for c in range(4)] for rows in spots]
+            totals = [[sums[tile, c, rows, :] for c in range(3)] for rows in spots]
             for entry in range(1, width):
                 partner = [partners[entry, c] for c in range(4)]
-                squared = squared_distance(own, partner)
-                distances[tile, entry, rows, :] = squared
-                terms = born_parts(squared, own[3], partner[3])
-                totals = [old + term for old, term in zip(totals, terms)]
-            sums[tile, 0, rows, :] = (
-                0.125 * totals[0] + 0.25 * totals[1] + (2.0 / own[3]) * totals[2]
-            )
+                for part, (rows, own) in enumerate(zip(spots, owns)):
+                    squared = squared_distance(own, partner)
+                    distances[tile, entry, rows, :] = squared
+                    terms = born_parts(squared, own[3], partner[3])
+                    totals[part] = [old + term for old, term in zip(totals[part], terms)]
+            for rows, own, total in zip(spots, owns, totals):
+                sums[tile, 0, rows, :] = (
+                    0.125 * total[0] + 0.25 * total[1] + (2.0 / own[3]) * total[2]
+                )
             return inner
 
-        lax.fori_loop(0, steps, one_step, 0, unroll=steps)
+        lax.fori_loop(0, steps // 4, one_step, 0, unroll=steps // 4)
         return carry
 
     lax.fori_loop(0, tiles, born_far, 0)
@@ -277,17 +279,20 @@
             )
 
         def one_step(step, inner):
-            rows = pl.ds(pl.multiple_of(step * ROWS, ROWS), ROWS)
-            own_column = born_columns[tile, 0, rows, :]
-            total = sums[tile, 0, rows, :]
+            spots = [pl.ds((step * 4 + part) * ROWS, ROWS) for part in range(4)]
+            own_columns = [born_columns[tile, 0, rows, :] for rows in spots]
+            totals = [sums[tile, 0, rows, :] for rows in spots]
             for entry in range(1, width):
-                total = total + energy_part(
-                    distances[tile, entry, rows, :], own_column, partners[entry, 0], partners[entry, 1]
-                )
-            sums[tile, 0, rows, :] = total
+                over, charge = partners[entry, 0], partners[entry, 1]
+                for part, rows in enumerate(spots):
+                    totals[part] = totals[part] + energy_part(
+                        distances[tile, entry, rows, :], own_columns[part], over, charge
+                    )
+            for rows, total in zip(spots, totals):
+                sums[tile, 0, rows, :] = total
             return inner
 
-        lax.fori_loop(0, steps, one_step, 0, unroll=steps)
+        lax.fori_loop(0, steps // 4, one_step, 0, unroll=steps // 4)
         return carry
 
     lax.fori_loop(0, tiles, energy_far, 0)

time: 37.3 us -> 37.5 us (level)
  no operation moved by 1% of the time
where the time goes in v9:
time: 37.5 us; the launch traced here: 37.2 us
  Pallas kernels  34.1 us (91%)
  between operations  3.02 us (8%)
    pallas_call x1, Pallas kernels, shards(): pl.pallas_call(functools.partial(kernel, count), out_shape=(block, block,...  32.8 us
    pallas_call x1, Pallas kernels, shards(): pl.pallas_call(hand_over, out_shape=(block, block), in_specs=[vmem] * 2,...  1.32 us

profile of v9, /device:TPU:0, one launch (start us, length us, event | category | flops | bytes accessed | tf_op | source)
XLA Modules:
  0.0 37.2 jit_solution(895838999259036818)
XLA Ops:
  1.3 32.8 %shard_map.94 = (f32[16,128]{1,0:T(8,128)}, f32[16,128]{1,0:T(8,128)}, f32[1,1]{1,0:T(1,128)}) custom-call(s32[8,16]{1,0:T(8,128)} %bitcast.10, s32[16]{0:T(128)} %counts_in.1, s32[1]{0:T(128)S(6)} %copy.11.fill_in, f32[3,2048]{1,0:T(4,128)} %coords_in.1, f32[16,128]{1,0:T(8,128)} %bitcast.7, f32[16,128]{1,0:T(8,128)} %bitcast.8, f32[16,128]{1,0:T(8,128)} %bitcast.9), custom_call_target="tpu_custom_call" | custom-call | tf_op jit(solution)/shard_map/pallas_call | solution.py:348
  34.1 1.3 %shard_map.95 = (f32[16,128]{1,0:T(8,128)}, f32[16,128]{1,0:T(8,128)}) custom-call(f32[16,128]{1,0:T(8,128)} %get-tuple-element.8.born, f32[16,128]{1,0:T(8,128)} %get-tuple-element.9.energy), custom_call_target="tpu_custom_call" | custom-call | tf_op jit(solution)/shard_map/pallas_call | solution.py:392

commit v10 on v5

--- a/solution.py
+++ b/solution.py
@@ -248,7 +248,7 @@
         lax.fori_loop(0, steps, one_step, 0, unroll=steps)
         return carry
 
-    lax.fori_loop(0, tiles, born_far, 0)
+    lax.fori_loop(0, tiles, born_far, 0, unroll=2)
 
     radius_own = jnp.where(live, radii[...], 1.5)
     psi = row_sums() * offset_own
@@ -306,7 +306,7 @@
         lax.fori_loop(0, steps, one_step, 0, unroll=steps)
         return carry
 
-    lax.fori_loop(0, tiles, energy_far, 0)
+    lax.fori_loop(0, tiles, energy_far, 0, unroll=4)
 
     energy = -0.5 * charge_window[home, :] * row_sums()
     energy_out[...] = energy
@@ -341,15 +341,9 @@
     lax.fori_loop(1, count, total_sent, 0)
 
 
-def hand_over(born, energy, born_out, energy_out, sems):
-    copies = [
-        pltpu.make_async_copy(born, born_out, sems.at[0]),
-        pltpu.make_async_copy(energy, energy_out, sems.at[1]),
-    ]
-    for copy in copies:
-        copy.start()
-    for copy in copies:
-        copy.wait()
+def hand_over(born, energy, born_out, energy_out):
+    born_out[...] = born[...]
+    energy_out[...] = energy[...]
 
 
 def solution(mesh):
@@ -409,9 +403,8 @@
         born, energy = pl.pallas_call(
             hand_over,
             out_shape=(block, block),
-            in_specs=[hbm] * 2,
-            out_specs=(hbm, hbm),
-            scratch_shapes=[pltpu.SemaphoreType.DMA((2,))],
+            in_specs=[vmem] * 2,
+            out_specs=(vmem, vmem),
         )(born, energy)
         return born.reshape(-1), energy.reshape(-1), total.reshape(())
 

time: 37.5 us -> 37 us (0.987)
  Pallas kernels: 34.2 us -> 33.6 us
where the time goes in v10:
time: 37 us; the launch traced here: 36.7 us
  Pallas kernels  33.6 us (91%)
  between operations  3.02 us (8%)
    pallas_call x1, Pallas kernels, shards(): pl.pallas_call(functools.partial(kernel, count), out_shape=(block, block,...  32.3 us
    pallas_call x1, Pallas kernels, shards(): pl.pallas_call(hand_over, out_shape=(block, block), in_specs=[vmem] * 2,...  1.32 us

profile of v10, /device:TPU:0, one launch (start us, length us, event | category | flops | bytes accessed | tf_op | source)
XLA Modules:
  0.0 36.7 jit_solution(13525399741154920666)
XLA Ops:
  1.3 32.3 %shard_map.94 = (f32[16,128]{1,0:T(8,128)}, f32[16,128]{1,0:T(8,128)}, f32[1,1]{1,0:T(1,128)}) custom-call(s32[8,16]{1,0:T(8,128)} %bitcast.10, s32[16]{0:T(128)} %counts_in.1, s32[1]{0:T(128)S(6)} %copy.11.fill_in, f32[3,2048]{1,0:T(4,128)} %coords_in.1, f32[16,128]{1,0:T(8,128)} %bitcast.7, f32[16,128]{1,0:T(8,128)} %bitcast.8, f32[16,128]{1,0:T(8,128)} %bitcast.9), custom_call_target="tpu_custom_call" | custom-call | tf_op jit(solution)/shard_map/pallas_call | solution.py:359
  33.6 1.3 %shard_map.95 = (f32[16,128]{1,0:T(8,128)}, f32[16,128]{1,0:T(8,128)}) custom-call(f32[16,128]{1,0:T(8,128)} %get-tuple-element.8.born, f32[16,128]{1,0:T(8,128)} %get-tuple-element.9.energy), custom_call_target="tpu_custom_call" | custom-call | tf_op jit(solution)/shard_map/pallas_call | solution.py:403
